TPU v7x, 32 devices: a whole 2x2x4 slice. The times are simulated.
32 devices in a mesh: groups: 2 (over y), ctx: 4 (over z), dp: 4 (over x, core).
Axes of the slice: x: 2, y: 2, z: 4, core: 2. Of those that a mesh axis runs over, the one named last changes fastest.
Arguments:
- layer_input: bfloat16 [8, 512, 4096], P(('groups', 'dp'), 'ctx'), parts along dimension 0, may hold values from -6 to 6
- head_input: bfloat16 [8, 512, 2048], P(('groups', 'dp'), 'ctx'), parts along dimension 0, may hold values from -6 to 6
- input_map: bfloat16 [8, 512, 64], P(('groups', 'dp'), 'ctx'), parts along dimension 0, may hold values from -2 to 2
- output_map: bfloat16 [8, 512, 64], P(('groups', 'dp'), 'ctx'), parts along dimension 0, may hold values from -0.25 to 0.25
- step_weight: bfloat16 [4096, 64], P(('ctx', 'dp')), may hold values from -0.09375 to 0.09375
- decay_log: float32 [64], replicated, may hold values from -9 to -3
- pack_place: int32 [8, 512], P(('groups', 'dp')), parts along dimension 0, may hold values from 0 to 511, as said below
- doc_starts: int32 [8, 512], P(('groups', 'dp'), 'ctx'), parts along dimension 0, may hold values from 0 to 1, as said below
- out_grad: bfloat16 [8, 512, 2048], P(('groups', 'dp'), 'ctx'), parts along dimension 0, may hold values from -1.5 to 1.5
Outputs:
- head_input_grad: bfloat16 [8, 512, 2048], P(('groups', 'dp'), 'ctx'), parts along dimension 0
- input_map_grad: float32 [8, 512, 64], P(('groups', 'dp'), 'ctx'), parts along dimension 0
- output_map_grad: float32 [8, 512, 64], P(('groups', 'dp'), 'ctx'), parts along dimension 0
- step_weight_grad: float32 [8192, 64], P(('groups', 'ctx', 'dp')), parts along dimension 0
There are 2 independent parts, one for each index of `groups`. A program takes and returns all parts, laid end to end along the dimension named above; an argument that names none is the same for every part. Nothing has to cross between parts.
Inputs may be any that keep to these rules, and one draw needn't show every extreme that they name: `pack_place`: each row is a permutation of the packed positions; of the 128 tokens at sampler positions k * 128 to (k + 1) * 128 - 1, exactly 32 land in each block of 128 packed positions. `doc_starts`: the first position of every row is 1.
All inputs are finite; a program needn't handle non-finite values.
Results may differ from a plain program's by a relative error of at most 0.0038.
Values may be sent and summed in bfloat16 or wider, within the bound.
A program may use at most 128 MiB of HBM per device.

v0:
```python
import jax
import jax.numpy as jnp
from jax import lax
from jax.sharding import PartitionSpec as P

HIGHEST_PRECISION = lax.Precision.HIGHEST


def carried_in(array, axis, combine, identity, reverse):
    size, mine = (lax.axis_size(axis), lax.axis_index(axis))
    everything = jax.tree.map(lambda part: lax.all_gather(part, axis), array)
    start = jax.tree.map(
        lambda part, zero: jnp.broadcast_to(jnp.asarray(zero, part.dtype), part.shape),
        array,
        identity,
    )

    def turn(k, before):
        at = size - 1 - k if reverse else k
        reached = at > mine if reverse else at < mine
        new = combine(before, jax.tree.map(lambda part: part[at], everything))
        return jax.tree.map(lambda a, b: jnp.where(reached, a, b), new, before)

    return lax.fori_loop(0, size, turn, start)


def contract(form, *operands):
    return jnp.einsum(form, *operands, precision=HIGHEST_PRECISION)


def chain_link(earlier, later):
    return (earlier[0] * later[0], later[1] + later[0][:, :, None, None] * earlier[1])


def route_slots(pack_place, block_len):
    shard_index = lax.axis_index("ctx")
    local_place = lax.dynamic_slice_in_dim(pack_place, shard_index * block_len, block_len, 1)
    sender_order = jnp.argsort(local_place, axis=1)
    targets = shard_index * block_len + jnp.arange(block_len, dtype=jnp.int32)
    all_positions = jnp.arange(pack_place.shape[1], dtype=jnp.int32)
    matches = pack_place[:, None, :] == targets[None, :, None]
    anchor = jnp.sum(jnp.where(matches, all_positions[None, None, :], 0), axis=2) // block_len
    positions = jnp.arange(block_len, dtype=jnp.int32)
    before = positions[None, :] < positions[:, None]
    same_anchor = (anchor[:, :, None] == anchor[:, None, :]) & before[None]
    rank_within = jnp.sum(same_anchor.astype(jnp.int32), axis=2)
    return (sender_order, anchor * (block_len // lax.axis_size("ctx")) + rank_within)


def on_device(
    layer_input,
    head_input,
    input_map,
    output_map,
    step_weight,
    decay_log,
    pack_place,
    doc_starts,
    out_grad,
):
    shard_count = lax.axis_size("ctx")
    rows_dev, block_len, inner_width = head_input.shape
    head_count = decay_log.shape[0]
    head_dim = inner_width // head_count
    model_dim = layer_input.shape[2]
    send_rows = block_len // shard_count
    sender_order, slot_index = route_slots(pack_place, block_len)

    def for_sending(array):
        ordered = jnp.take_along_axis(array, sender_order[:, :, None], axis=1)
        return ordered.reshape(rows_dev, shard_count, send_rows, array.shape[2])

    def packed_order(received):
        flat_rows = received.reshape(rows_dev, block_len, received.shape[3])
        return jnp.take_along_axis(flat_rows, slot_index[:, :, None], axis=1)

    flat_rows = layer_input.reshape(rows_dev * block_len, model_dim)
    columns = flat_rows
    summed = jnp.dot(
        columns,
        lax.all_gather(step_weight, ("ctx", "dp"), axis=0, tiled=True),
        preferred_element_type=jnp.float32,
    )
    raw_local = lax.optimization_barrier(summed.astype(jnp.bfloat16)).reshape(
        rows_dev, block_len, head_count
    )
    received = (
        lax.all_to_all(for_sending(head_input), "ctx", split_axis=1, concat_axis=1, tiled=True),
        lax.all_to_all(for_sending(input_map), "ctx", split_axis=1, concat_axis=1, tiled=True),
        lax.all_to_all(for_sending(output_map), "ctx", split_axis=1, concat_axis=1, tiled=True),
        lax.all_to_all(for_sending(raw_local), "ctx", split_axis=1, concat_axis=1, tiled=True),
    )
    x_packed = packed_order(received[0])
    b_packed = packed_order(received[1])
    c_packed = packed_order(received[2])
    raw_packed = packed_order(received[3])
    decay_rate = jnp.exp(decay_log)
    raw_step = raw_packed.astype(jnp.float32)
    step_size = jax.nn.softplus(raw_step)
    log_decay = -step_size * decay_rate[None, None, :]
    cumul = jnp.cumsum(log_decay, axis=1)
    segment = jnp.cumsum(doc_starts, axis=1)
    alive = (segment == 0).astype(jnp.float32)
    positions = jnp.arange(block_len, dtype=jnp.int32)
    causal = positions[:, None] >= positions[None, :]
    joined = ((segment[:, :, None] == segment[:, None, :]) & causal[None])[:, None]
    cumul_heads = jnp.transpose(cumul, (0, 2, 1))
    spread = cumul_heads[:, :, :, None] - cumul_heads[:, :, None, :]
    kernel = jnp.where(joined, jnp.exp(jnp.where(joined, spread, 0.0)), 0.0)
    x_heads = x_packed.astype(jnp.float32).reshape(rows_dev, block_len, head_count, head_dim)
    b_full = b_packed.astype(jnp.float32)
    c_full = c_packed.astype(jnp.float32)
    scaled = x_heads * step_size[:, :, :, None]
    gram = contract("rin,rjn->rij", c_full, b_full)
    weighted = kernel * gram[:, None]
    enter = jnp.exp(cumul) * alive[:, :, None]
    tail_mask = (segment == segment[:, -1:]).astype(jnp.float32)
    leave = jnp.exp(cumul[:, -1:, :] - cumul) * tail_mask[:, :, None]
    end_state = contract("rjh,rjhp,rjn->rhpn", leave, scaled, b_full)
    decay_total = jnp.exp(cumul[:, -1, :]) * alive[:, -1:]
    identity = (jnp.ones_like(decay_total), jnp.zeros_like(end_state))
    state_in = carried_in((decay_total, end_state), "ctx", chain_link, identity, False)[1]
    cotangent = out_grad.astype(jnp.float32).reshape(rows_dev, block_len, head_count, head_dim)
    local_back = contract("rih,rihp,rin->rhpn", enter, cotangent, c_full)
    state_grad = carried_in((decay_total, local_back), "ctx", chain_link, identity, True)[1]
    grad_scaled = contract("rhij,rihp->rjhp", weighted, cotangent) + contract(
        "rjh,rhpn,rjn->rjhp", leave, state_grad, b_full
    )
    grad_weighted = contract("rihp,rjhp->rhij", cotangent, scaled)
    grad_gram = jnp.sum(kernel * grad_weighted, axis=1)
    product = weighted * grad_weighted
    grad_cumul = jnp.transpose(jnp.sum(product, axis=3) - jnp.sum(product, axis=2), (0, 2, 1))
    readout = contract("rhpn,rin->rihp", state_in, c_full)
    grad_cumul = grad_cumul + enter * jnp.sum(cotangent * readout, axis=3)
    flow = contract("rjhp,rhpn,rjn->rjh", scaled, state_grad, b_full) * leave
    grad_cumul = grad_cumul - flow
    last_extra = jnp.sum(flow, axis=1) + decay_total * jnp.sum(state_grad * state_in, axis=(2, 3))
    grad_cumul = grad_cumul.at[:, -1, :].add(last_extra)
    grad_log = jnp.flip(jnp.cumsum(jnp.flip(grad_cumul, 1), axis=1), 1)
    grad_step = jnp.sum(x_heads * grad_scaled, axis=3) - decay_rate[None, None, :] * grad_log
    grad_raw = grad_step * jax.nn.sigmoid(raw_step)
    head_grad = (
        (grad_scaled * step_size[:, :, :, None])
        .reshape(rows_dev, block_len, inner_width)
        .astype(jnp.bfloat16)
    )
    grad_c = contract("rij,rjn->rin", grad_gram, b_full) + contract(
        "rih,rihp,rhpn->rin", enter, cotangent, state_in
    )
    grad_b = contract("rij,rin->rjn", grad_gram, c_full) + contract(
        "rjh,rjhp,rhpn->rjn", leave, scaled, state_grad
    )
    inverse_slot = jnp.argsort(slot_index, axis=1)
    arranged = jnp.take_along_axis(grad_raw, inverse_slot[:, :, None], axis=1).reshape(
        rows_dev, shard_count, send_rows, head_count
    )
    returned = lax.all_to_all(arranged, "ctx", split_axis=1, concat_axis=1, tiled=True).reshape(
        rows_dev, block_len, head_count
    )
    inverse_order = jnp.argsort(sender_order, axis=1)
    grad_rows = jnp.take_along_axis(returned, inverse_order[:, :, None], axis=1)
    source_rows = layer_input.reshape(rows_dev * block_len, model_dim)
    grad_flat = grad_rows.reshape(rows_dev * block_len, head_count)
    columns = source_rows.astype(jnp.float32)
    weight_grad = lax.psum_scatter(
        lax.dot_general(columns, grad_flat, (((0,), (0,)), ((), ())), precision=HIGHEST_PRECISION),
        ("ctx", "dp"),
        scatter_dimension=0,
        tiled=True,
    )
    return (head_grad, grad_b, grad_c, weight_grad)


def solution(mesh):
    placed = (
        P(("groups", "dp"), "ctx", None),
        P(("groups", "dp"), "ctx", None),
        P(("groups", "dp"), "ctx", None),
        P(("groups", "dp"), "ctx", None),
        P(("ctx", "dp"), None),
        P(),
        P(("groups", "dp"), None),
        P(("groups", "dp"), "ctx"),
        P(("groups", "dp"), "ctx", None),
    )
    return jax.shard_map(
        on_device,
        mesh=mesh,
        in_specs=placed,
        out_specs=(
            P(("groups", "dp"), "ctx", None),
            P(("groups", "dp"), "ctx", None),
            P(("groups", "dp"), "ctx", None),
            P(("groups", "ctx", "dp"), None),
        ),
        check_vma=False,
    )
```

profile of v0, /device:TPU:0, one launch (start us, length us, event | category | flops | bytes accessed | tf_op | source)
XLA Modules:
  0.0 340.1 jit_solution(11761397503699112720)
XLA Ops:
  7.2 1.2 constant_dynamic-slice_fusion
  9.0 0.9 select_reduce_fusion
  10.1 24.8 %all_gather.21 = bf16[4096,64]{0,1:T(8,128)(2,1)S(1)} all-gather(bf16[256,64]{0,1:T(8,128)(2,1)} %param.25), channel_id=1, replica_groups=mesh['groups'=2,'ctx'=4,'dp'=4] {'ctx','dp'}, dimensions={0}, use_global_device_ids=true | all-gather | bytes 557056 | tf_op jit(solution)/shard_map/all_gather | solution.py:81
  34.9 1.0 reduce_window_sum.30
  37.8 0.9 copy.185
  38.6 0.8 copy.187
  40.7 0.7 gather_fusion
  43.6 3.3 all-to-all-start
  47.5 1.3 copy.190
  48.9 0.8 reshape.1065
  49.6 2.8 all-to-all-done
  52.4 3.3 all-to-all-start.1
  56.9 4.4 %all-to-all-done.1 = bf16[4,2,1024]{2,1,0:T(2,128)(2,1)S(1)} async-done(((bf16[4,2,1024]{2,1,0:T(2,128)(2,1)}), bf16[4,2,1024]{2,1,0:T(2,128)(2,1)S(1)}, u32[]{:S(2)}, u32[]{:S(2)}) %all-to-all-start.1) | async-done | bytes 16416 | tf_op jit(solution)/shard_map/all_to_all | solution.py:90
  61.4 0.7 gather_fusion.3
  62.3 2.2 fusion.28
  64.6 0.9 gather_fusion.6
  66.2 3.3 all-to-all-start.2
  69.5 0.9 bitcast_select_fusion.1
  70.4 4.8 %all-to-all-done.2 = bf16[4,2,1024]{2,1,0:T(2,128)(2,1)S(1)} async-done(((bf16[4,2,1024]{2,1,0:T(2,128)(2,1)}), bf16[4,2,1024]{2,1,0:T(2,128)(2,1)S(1)}, u32[]{:S(2)}, u32[]{:S(2)}) %all-to-all-start.2) | async-done | bytes 16416 | tf_op jit(solution)/shard_map/all_to_all | solution.py:89
  75.2 4.3 %all-to-all-start.3 = ((bf16[1,4,32,2048]{3,2,0,1:T(8,128)(2,1)}), bf16[1,4,32,2048]{3,2,0,1:T(8,128)(2,1)S(1)}, u32[]{:S(2)}, u32[]{:S(2)}) async-start(bf16[1,4,32,2048]{3,2,0,1:T(8,128)(2,1)} %bitcast.65), calls=%async_computation.3 | async-start | bytes 1048576 | tf_op jit(solution)/shard_map/all_to_all | solution.py:88
  83.1 0.7 gather_fusion.5
  83.8 18.1 %all_gather.24 = f32[4,1,64]{2,1,0:T(1,128)S(1)} all-gather(f32[1,1,64]{2,1,0:T(1,128)S(1)} %copy.197), channel_id=1, replica_groups=mesh['groups'=2,'ctx'=4,'dp'=4] {'ctx'}, dimensions={0}, use_global_device_ids=true | all-gather | bytes 1280 | tf_op jit(solution)/shard_map/all_gather | solution.py:11
  101.9 3.6 %all-to-all-done.3 = bf16[1,4,32,2048]{3,2,0,1:T(8,128)(2,1)S(1)} async-done(((bf16[1,4,32,2048]{3,2,0,1:T(8,128)(2,1)}), bf16[1,4,32,2048]{3,2,0,1:T(8,128)(2,1)S(1)}, u32[]{:S(2)}, u32[]{:S(2)}) %all-to-all-start.3) | async-done | bytes 524320 | tf_op jit(solution)/shard_map/all_to_all | solution.py:88
  105.5 1.7 gather_fusion.7
  107.2 1.2 fusion.35
  108.4 1.4 copy.204
  109.8 1.4 broadcast_multiply_fusion
  111.2 42.9 %all-gather.5.cloned.1.call-done = f32[256,32,64]{2,1,0:T(8,128)} async-done(((f32[64,32,64]{2,1,0:T(8,128)}), f32[256,32,64]{2,1,0:T(8,128)}) %all-gather.5.cloned.1.call-update) | async-done | bytes 2097168 | tf_op jit(solution)/shard_map/all_gather | solution.py:11
  154.1 6.1 %while.31 = (s32[]{:T(128)}, f32[1,64,32,64]{3,2,1,0:T(8,128)S(1)}, s32[]{:T(128)}, f32[4,1,64,32,64]{4,3,2,1,0:T(8,128)}, f32[4,1,64]{2,1,0:T(1,128)S(1)}, /*index=5*/s32[]{:T(128)}, s32[]{:T(128)}, s32[]{:T(128)}, s32[]{:T(128)}) while((s32[]{:T(128)}, f32[1,64,32,64]{3,2,1,0:T(8,128)S(1)}, s32[]{:T(128)}, ...), condition=%wide.region_6.8_spmd.clone, body=%wide.region_5.7_spmd.clone.sunk | while | flops 524296 | bytes 1573807 | solution.py:24
  154.1 1.5 fusion.83
  155.6 1.5 fusion.83
  157.1 1.5 fusion.83
  158.7 1.5 fusion.83
  160.2 2.9 multiply_reduce_fusion
  163.7 1.7 fusion.32
  166.8 1.2 and_bitcast_fusion.1
  168.0 1.1 fusion.70
  169.2 1.1 and_bitcast_fusion
  170.6 8.0 %fusion.6 = (f32[64,128]{1,0:T(8,128)}, f32[64,128]{1,0:T(8,128)}, f32[128,128]{0,1:T(8,128)}) fusion(f32[128,128]{0,1:T(8,128)S(1)} %fusion.61, f32[64,128]{1,0:T(8,128)S(1)} %copy.183, pred[128,128]{0,1:T(8,128)(4,1)} %fusion.48, f32[128,64,32]{0,2,1:T(8,128)} %copy-done.2, bf16[128,64,32]{0,2,1:T(8,128)(2,1)} %bitcast.340), kind=kOutput, calls=%fused_computation.23 | convolution fusion | flops 412057600 | bytes 1818624 | tf_op jit(solution)/shard_map/rihp,rjhp->rhij/dot_general | solution.py:28
  178.6 6.2 %multiply_reduce_fusion.2 = (f32[128,64]{0,1:T(8,128)}, bf16[1,128,64,32]{1,3,2,0:T(8,128)(2,1)}) fusion(f32[1,128,64,32]{1,3,2,0:T(8,128)S(1)} %bitcast.348, f32[128,64]{0,1:T(8,128)S(1)} %copy.202, f32[128,64,32]{0,1,2:T(8,128)S(1)} %copy-done.6, f32[128,64]{0,1:T(8,128)S(1)} %get-tuple-element.399, bf16[128,64,32]{0,2,1:T(8,128)(2,1)S(1)} %bitcast.343, ...), kind=kOutput, calls=%fused_computation.51 | convolution fusion | flops 408412160 | bytes 3358720 | tf_op jit(solution)/shard_map/rhij,rihp->rjhp/dot_general | solution.py:28
  184.8 0.8 copy.210
  186.3 58.3 %all-gather.7.cloned.1.call-done = f32[256,32,64]{2,1,0:T(8,128)} async-done(((f32[64,32,64]{2,1,0:T(8,128)}), f32[256,32,64]{2,1,0:T(8,128)}) %all-gather.7.cloned.1.call-update) | async-done | bytes 2097168 | tf_op jit(solution)/shard_map/all_gather | solution.py:11
  244.7 8.5 %while.32 = (s32[]{:T(128)}, f32[1,64,32,64]{3,2,1,0:T(8,128)S(1)}, s32[]{:T(128)}, f32[4,1,64,32,64]{4,3,2,1,0:T(8,128)}, f32[4,1,64]{2,1,0:T(1,128)}, /*index=5*/s32[]{:T(128)}, s32[]{:T(128)}) while((s32[]{:T(128)}, f32[1,64,32,64]{3,2,1,0:T(8,128)S(1)}, s32[]{:T(128)}, f32[4,1,64,32,64]{4,3,2,1,0:T(8,128)}, ...), condition=%wide.region_9.12_spmd.clone, body=%wide.region_8.11_spmd.clone.sunk | while | flops 524292 | bytes 1573745 | solution.py:24
  245.3 1.5 fusion.84
  247.5 1.5 fusion.84
  249.6 1.5 fusion.84
  251.7 1.5 fusion.84
  253.8 3.0 fusion.19
  257.5 0.9 fusion.51
  258.4 0.8 slice_add_fusion
  259.8 0.8 reduce_window_sum.33
  260.6 0.8 rev.8
  261.4 0.8 fusion.42
  263.5 0.7 reshape.1071
  264.3 3.3 all-to-all-start.4
  268.2 5.0 %all-to-all-done.4 = f32[4,1,2048]{2,1,0:T(1,128)S(1)} async-done(((f32[4,1,2048]{2,1,0:T(1,128)}), f32[4,1,2048]{2,1,0:T(1,128)S(1)}, u32[]{:S(2)}, u32[]{:S(2)}) %all-to-all-start.4) | async-done | bytes 32800 | tf_op jit(solution)/shard_map/all_to_all | solution.py:157
  273.7 0.7 reduce.20
  275.1 2.3 convolution_bitcast_fusion
  277.4 1.1 fusion.63
  278.6 1.1 fusion.59
  279.7 2.0 copy.218
  281.7 3.7 %fusion.23 = f32[1,128,64]{1,2,0:T(8,128)} fusion(f32[128,64]{0,1:T(8,128)S(1)} %fusion.63, f32[128,64,32]{0,2,1:T(8,128)} %copy-done.2, f32[128,64]{0,1:T(8,128)S(1)} %get-tuple-element.399, f32[1,64,32,64]{3,2,1,0:T(8,128)S(1)} %get-tuple-element.249), kind=kOutput, calls=%fused_computation.40 | convolution fusion | flops 201596928 | bytes 1671168 | tf_op jit(solution)/shard_map/rjh,rjhp,rhpn->rjn/dot_general | solution.py:28
  285.5 4.2 %fusion.21 = f32[1,128,64]{1,2,0:T(8,128)} fusion(f32[128,64]{0,1:T(8,128)S(1)} %fusion.59, f32[64,32,64]{2,1,0:T(8,128)S(1)} %bitcast.335, f32[128,64]{0,1:T(8,128)S(1)} %fusion.58, bf16[128,64,32]{0,2,1:T(8,128)(2,1)} %bitcast.342), kind=kOutput, calls=%fused_computation.37 | convolution fusion | flops 201859072 | bytes 1146880 | tf_op jit(solution)/shard_map/rih,rihp,rhpn->rin/dot_general | solution.py:28
  289.7 43.6 %reduce-scatter.2.cloned.1.call-done = f32[256,64]{0,1:T(8,128)} async-done(((f32[4096,64]{0,1:T(8,128)}), f32[256,64]{0,1:T(8,128)}) %reduce-scatter.2.cloned.1.call-update) | async-done | bytes 65552 | tf_op jit(solution)/shard_map/reduce_scatter | solution.py:165
  (102 shorter events, 22.5 us)
Async XLA Ops:
  7.2 29.3 %copy-start = (bf16[1,128,4096]{2,1,0:T(8,128)(2,1)S(1)}, bf16[1,128,4096]{2,1,0:T(8,128)(2,1)}, u32[]{:S(2)}) copy-start(bf16[1,128,4096]{2,1,0:T(8,128)(2,1)} %param.21) | copy-start | bytes 3145732
  7.2 32.3 %sort.32.cloned.1.call-start = ((), (), s32[]{:S(2)}) async-start(), calls=%async_computation.9 | async-start | bytes 3104 | tf_op jit(solution)/shard_map/jit(argsort)/sort | solution.py:38
  37.6 26.9 %copy-start.8 = (f32[128]{0:T(128)}, f32[128]{0:T(128)S(1)}, u32[]{:S(2)}) copy-start(f32[128]{0:T(128)S(1)} %get-tuple-element.405) | copy-start | bytes 1540
  37.7 26.8 %copy-start.1 = (bf16[1,128,2048]{2,1,0:T(8,128)(2,1)S(1)}, bf16[1,128,2048]{2,1,0:T(8,128)(2,1)}, u32[]{:S(2)}) copy-start(bf16[1,128,2048]{2,1,0:T(8,128)(2,1)} %param.22) | copy-start | bytes 1572868
  43.6 8.8 %all-to-all-start = ((bf16[4,2,1024]{2,1,0:T(2,128)(2,1)}), bf16[4,2,1024]{2,1,0:T(2,128)(2,1)S(1)}, u32[]{:S(2)}, u32[]{:S(2)}) async-start(bf16[4,2,1024]{2,1,0:T(2,128)(2,1)} %reshape.1069), calls=%async_computation | async-start | bytes 32768 | tf_op jit(solution)/shard_map/all_to_all | solution.py:91
  47.5 18.0 %copy-start.9 = (f32[64]{0:T(128)}, f32[64]{0:T(128)S(1)}, u32[]{:S(2)}) copy-start(f32[64]{0:T(128)S(1)} %exp.49) | copy-start | bytes 772
  48.9 16.7 %copy-start.3 = (bf16[1,128,2048]{1,2,0:T(8,128)(2,1)}, bf16[1,128,2048]{1,2,0:T(8,128)(2,1)S(1)}, u32[]{:S(2)}) copy-start(bf16[1,128,2048]{1,2,0:T(8,128)(2,1)S(1)} %copy.190) | copy-start | bytes 1572868
  52.4 8.8 %all-to-all-start.1 = ((bf16[4,2,1024]{2,1,0:T(2,128)(2,1)}), bf16[4,2,1024]{2,1,0:T(2,128)(2,1)S(1)}, u32[]{:S(2)}, u32[]{:S(2)}) async-start(bf16[4,2,1024]{2,1,0:T(2,128)(2,1)} %reshape.1065), calls=%async_computation.1 | async-start | bytes 32768 | tf_op jit(solution)/shard_map/all_to_all | solution.py:90
  55.7 98.3 %all-gather.5.cloned.1.call-start = ((), (), s32[]{:S(2)}) async-start(), calls=%async_computation.7 | async-start | bytes 5242880 | tf_op jit(solution)/shard_map/all_gather | solution.py:11
  66.2 8.9 %all-to-all-start.2 = ((bf16[4,2,1024]{2,1,0:T(2,128)(2,1)}), bf16[4,2,1024]{2,1,0:T(2,128)(2,1)S(1)}, u32[]{:S(2)}, u32[]{:S(2)}) async-start(bf16[4,2,1024]{2,1,0:T(2,128)(2,1)} %reshape.1067), calls=%async_computation.2 | async-start | bytes 32768 | tf_op jit(solution)/shard_map/all_to_all | solution.py:89
  75.2 30.3 %all-to-all-start.3 = ((bf16[1,4,32,2048]{3,2,0,1:T(8,128)(2,1)}), bf16[1,4,32,2048]{3,2,0,1:T(8,128)(2,1)S(1)}, u32[]{:S(2)}, u32[]{:S(2)}) async-start(bf16[1,4,32,2048]{3,2,0,1:T(8,128)(2,1)} %bitcast.65), calls=%async_computation.3 | async-start | bytes 1048576 | tf_op jit(solution)/shard_map/all_to_all | solution.py:88
  79.5 86.6 %sort.43.cloned.1.call-start = ((), (), s32[]{:S(2)}) async-start(), calls=%async_computation.10 | async-start | bytes 3104 | tf_op jit(solution)/shard_map/jit(argsort)/sort | solution.py:153
  80.7 87.3 %sort.45.cloned.1.call-start = ((), (), s32[]{:S(2)}) async-start(), calls=%async_computation.11 | async-start | bytes 3104 | tf_op jit(solution)/shard_map/jit(argsort)/sort | solution.py:160
  82.6 162.1 %all-gather.7.cloned.1.call-start = ((), (), s32[]{:S(2)}) async-start(), calls=%async_computation.8 | async-start | bytes 5242880 | tf_op jit(solution)/shard_map/all_gather | solution.py:11
  111.1 52.6 %copy-start.2 = (f32[128,64,32]{0,2,1:T(8,128)}, f32[128,64,32]{0,2,1:T(8,128)S(1)}, u32[]{:S(2)}) copy-start(f32[128,64,32]{0,2,1:T(8,128)S(1)} %broadcast_multiply_fusion) | copy-start | bytes 3145732
  160.2 6.0 %copy-start.10 = (f32[4,1,64]{2,1,0:T(1,128)}, f32[4,1,64]{2,1,0:T(1,128)S(1)}, u32[]{:S(2)}) copy-start(f32[4,1,64]{2,1,0:T(1,128)S(1)} %get-tuple-element.549) | copy-start | bytes 3076
  170.6 8.0 %copy-start.4 = (bf16[1,128,2048]{1,2,0:T(8,128)(2,1)S(1)}, bf16[1,128,2048]{1,2,0:T(8,128)(2,1)}, u32[]{:S(2)}) copy-start(bf16[1,128,2048]{1,2,0:T(8,128)(2,1)} %copy-done.3) | copy-start | bytes 1572868
  170.6 8.0 %copy-start.5 = (f32[1,128,2048]{1,2,0:T(8,128)S(1)}, f32[1,128,2048]{1,2,0:T(8,128)}, u32[]{:S(2)}) copy-start(f32[1,128,2048]{1,2,0:T(8,128)} %copy.204) | copy-start | bytes 3145732
  170.6 8.0 %copy-start.6 = (f32[128,64,32]{0,1,2:T(8,128)S(1)}, f32[128,64,32]{0,1,2:T(8,128)}, u32[]{:S(2)}) copy-start(f32[128,64,32]{0,1,2:T(8,128)} %get-tuple-element.410) | copy-start | bytes 3145732
  170.6 8.0 %copy-start.7 = (pred[128,128]{0,1:T(8,128)(4,1)S(1)}, pred[128,128]{0,1:T(8,128)(4,1)}, u32[]{:S(2)}) copy-start(pred[128,128]{0,1:T(8,128)(4,1)} %fusion.48) | copy-start | bytes 49156
  264.3 8.9 %all-to-all-start.4 = ((f32[4,1,2048]{2,1,0:T(1,128)}), f32[4,1,2048]{2,1,0:T(1,128)S(1)}, u32[]{:S(2)}, u32[]{:S(2)}) async-start(f32[4,1,2048]{2,1,0:T(1,128)} %reshape.1071), calls=%async_computation.4 | async-start | bytes 65536 | tf_op jit(solution)/shard_map/all_to_all | solution.py:157
  267.5 65.8 %reduce-scatter.2.cloned.1.call-start = ((), (), s32[]{:S(2)}) async-start(), calls=%async_computation.6 | async-start | bytes 1114112 | tf_op jit(solution)/shard_map/reduce_scatter | solution.py:165
Sparse Core Ops, SparseCore 0:
  10.8 2.2 sort.47.cloned.1.call-done
  64.7 89.3 all-gather.4
  156.4 2.2 sort.49.cloned.1.call-done
  161.5 2.2 sort.51.cloned.1.call-done
  165.5 79.0 all-gather.6
  277.5 55.6 reduce-scatter.1
  (3 shorter events, 0.0 us)
where the time goes:
time: 342 us; the launch traced here: 340 us
  waiting for transfers between devices  165 us (48%)
  blocking collectives  42.9 us (13%)
  matrix products  37.1 us (11%)
  other arithmetic  31.9 us (9%)
  local copies, waits for them, and re-layouts  29.9 us (9%)
  starting transfers between devices  17.5 us (5%)
  between operations  15.2 us (4%)
    all_gather x2, waiting for transfers between devices, carried_in(): everything = jax.tree.map(lambda part: lax.all_gather(part, axis), array)  101 us
    reduce_scatter x1, waiting for transfers between devices, on_device(): lax.psum_scatter(lax.dot_general(columns, grad_flat, (((0,), (0,)), ((),...  43.6 us
    dot_general x11, matrix products, contract(): return jnp.einsum(form, *operands, precision=HIGHEST_PRECISION)  34.4 us
    all_gather x1, blocking collectives, on_device(): lax.all_gather(step_weight, ('ctx', 'dp'), axis=0, tiled=True)  24.8 us
    all_gather x1, blocking collectives, carried_in(): everything = jax.tree.map(lambda part: lax.all_gather(part, axis), array)  18.1 us
    select_n x8, other arithmetic, turn(): return jax.tree.map(lambda a, b: jnp.where(reached, a, b), new, before)  11.9 us
    unnamed x37, local copies, waits for them, and re-layouts  8.47 us
  transfers between devices with their start and end apart: 8, of which 8 were waited for; matrix products, arithmetic and copies ran while one was open for 14% of the time, Pallas kernels for 0%

commit v1 on v0

--- a/solution.py
+++ b/solution.py
@@ -1,6 +1,10 @@
+import functools
+
 import jax
 import jax.numpy as jnp
 from jax import lax
+from jax.experimental import pallas as pl
+from jax.experimental.pallas import tpu as pltpu
 from jax.sharding import PartitionSpec as P
 
 HIGHEST_PRECISION = lax.Precision.HIGHEST
@@ -171,6 +175,519 @@
     return (head_grad, grad_b, grad_c, weight_grad)
 
 
+def mm(a, b):
+    return jnp.dot(a, b, preferred_element_type=jnp.float32)
+
+
+def nt(a, b, precision=None):
+    return lax.dot_general(
+        a, b, (((1,), (1,)), ((), ())), precision=precision, preferred_element_type=jnp.float32
+    )
+
+
+def one_hot(mask, kind=jnp.bfloat16):
+    return jnp.where(mask, 1.0, 0.0).astype(kind)
+
+
+def iotas(rows, columns):
+    return (
+        lax.broadcasted_iota(jnp.int32, (rows, columns), 0),
+        lax.broadcasted_iota(jnp.int32, (rows, columns), 1),
+    )
+
+
+def eye(size, kind=jnp.bfloat16):
+    row, column = iotas(size, size)
+    return one_hot(row == column, kind)
+
+
+def two_parts(array):
+    high = array.astype(jnp.bfloat16)
+    return high, (array - high.astype(jnp.float32)).astype(jnp.bfloat16)
+
+
+def remote(src, dst, send_sem, recv_sem, **where):
+    return pltpu.make_async_remote_copy(
+        src_ref=src,
+        dst_ref=dst,
+        send_sem=send_sem,
+        recv_sem=recv_sem,
+        device_id=where,
+        device_id_type=pl.DeviceIdType.MESH,
+    )
+
+
+def layer_kernel(
+    dims,
+    u_ref, x_ref, b_ref, c_ref, w_ref, log_ref, place_ref, start_ref, g_ref,
+    dx_ref, db_ref, dc_ref, dw_ref,
+    wall, us, uall, xs, xr, bcs, bcr, raws, rawr, xp,
+    step_wide, enter_wide, leave_wide, y_acc, gs_acc, eg, lx,
+    end_own, back_own, end_all, f_out, f_in, g_out, g_in,
+    cum_col, cum_row, step_row, gram_grad, gsl, gall, ps, pr,
+    wz_s, wz_r, wd_s, wd_r, u_s, u_r, x_s, x_r, bc_s, bc_r, raw_s, raw_r,
+    f_s, f_r, b_s, b_r, g_s, g_r, p_s, p_r,
+):
+    n, m, length, heads, head_dim, state, chunks = dims
+    f32, bf = jnp.float32, jnp.bfloat16
+    me, mine = lax.axis_index("ctx"), lax.axis_index("dp")
+    rows = length // n
+    block = w_ref.shape[0]
+    width = heads * head_dim
+    wide = width // chunks
+    per = 128 // head_dim
+
+    def z_peer(k):
+        return lax.rem(me + k, n)
+
+    def d_peer(k):
+        return lax.rem(mine + k, m)
+
+    def piece(k):
+        return pl.ds(pl.multiple_of(k * rows, rows), rows)
+
+    barrier = pltpu.get_barrier_semaphore()
+    for kz in range(n):
+        for kd in range(m):
+            if kz or kd:
+                pl.semaphore_signal(
+                    barrier, inc=1, device_id={"ctx": z_peer(kz), "dp": d_peer(kd)},
+                    device_id_type=pl.DeviceIdType.MESH,
+                )
+
+    wall[mine, me] = nt(eye(heads), w_ref[...]).astype(bf)
+    row, column = iotas(length, length)
+    row_f = row.astype(f32)
+    before = one_hot(row < column)
+    lower = one_hot(row >= column)
+
+    def prefix(flags):
+        return mm(jnp.broadcast_to(flags, (8, length)).astype(bf), before)[0:1]
+
+    own_place = jnp.zeros((1, length), jnp.int32)
+    for k in range(n):
+        own_place = jnp.where(me == k, place_ref[:, k * length : (k + 1) * length], own_place)
+    slot = jnp.zeros((1, length), f32)
+    for k in range(n):
+        flags = one_hot((own_place >= k * length) & (own_place < (k + 1) * length), f32)
+        slot = slot + flags * (k * rows + prefix(flags))
+    p_send = one_hot(slot == row_f)
+    pl.semaphore_wait(barrier, n * m - 1)
+
+    w_z = []
+    for k in range(1, n):
+        copy = remote(
+            wall.at[mine, me], wall.at[mine, me], wz_s.at[k], wz_r.at[k], ctx=z_peer(k), dp=mine
+        )
+        copy.start()
+        w_z.append(copy)
+
+    xs[...] = mm(p_send, x_ref[...]).astype(bf)
+    bcs[0] = mm(p_send, b_ref[...]).astype(bf)
+    bcs[1] = mm(p_send, c_ref[...]).astype(bf)
+    x_copies, bc_copies = [], []
+    for k in range(1, n):
+        to = z_peer(k)
+        copy = remote(
+            bcs.at[:, piece(to)], bcr.at[:, piece(me)], bc_s.at[k], bc_r.at[k], ctx=to, dp=mine
+        )
+        copy.start()
+        bc_copies.append(copy)
+    for k in range(1, n):
+        to = z_peer(k)
+        copy = remote(xs.at[piece(to)], xr.at[piece(me)], x_s.at[k], x_r.at[k], ctx=to, dp=mine)
+        copy.start()
+        x_copies.append(copy)
+    bcr[:, piece(me)] = bcs[:, piece(me)]
+    xr[piece(me)] = xs[piece(me)]
+
+    for copy in w_z:
+        copy.wait_recv()
+    w_d = []
+    for k in range(1, m):
+        copy = remote(
+            wall.at[mine], wall.at[mine], wd_s.at[k], wd_r.at[k], ctx=me, dp=d_peer(k)
+        )
+        copy.start()
+        w_d.append(copy)
+
+    for d in range(m):
+        for z in range(n):
+            at = (z * m + d) * block
+            us[d, :, z * block : (z + 1) * block] = mm(
+                p_send, u_ref[:, at : at + block]
+            ).astype(bf)
+    u_copies = []
+    for k in range(1, m):
+        to = d_peer(k)
+        copy = remote(us.at[to], uall.at[mine], u_s.at[k], u_r.at[k], ctx=me, dp=to)
+        copy.start()
+        u_copies.append(copy)
+    uall[mine] = us[mine]
+
+    p_recv = jnp.zeros((length, length), f32)
+    p_back = jnp.zeros((length, length), f32)
+    for k in range(n):
+        place = place_ref[:, k * length : (k + 1) * length] - me * length
+        here = (place >= 0) & (place < length)
+        rank = jnp.where(here, k * rows + prefix(one_hot(here, f32)), -1.0)
+        lands = one_hot(place == row)
+        comes = one_hot(rank == row_f)
+        p_recv = p_recv + nt(lands, comes)
+        p_back = p_back + nt(comes, lands)
+    p_recv, p_back = p_recv.astype(bf), p_back.astype(bf)
+
+    starts = jnp.broadcast_to(start_ref[...].astype(f32), (8, length)).astype(bf)
+    seg_col = nt(lower, starts)[:, 0:1]
+    seg_row = nt(starts, lower)[0:1]
+    seg_last = seg_row[:, length - 1 : length]
+    joined = (seg_col == seg_row) & (row >= column)
+    joined_t = (seg_col == seg_row) & (row <= column)
+    alive = one_hot(seg_col == 0.0, f32)
+    tail = one_hot(seg_col == seg_last, f32)
+    alive_last = one_hot(seg_last == 0.0, f32)
+
+    raw = jnp.zeros((length, heads), f32)
+    for k in range(m):
+        if k:
+            w_d[k - 1].wait_recv()
+        part = lax.rem(mine + m - k, m)
+        for z in range(n):
+            raw = raw + nt(us[part, :, z * block : (z + 1) * block], wall[part, z])
+    raws[...] = raw.astype(bf)
+    raw_copies = []
+    for k in range(1, n):
+        to = z_peer(k)
+        copy = remote(
+            raws.at[piece(to)], rawr.at[piece(me)], raw_s.at[k], raw_r.at[k], ctx=to, dp=mine
+        )
+        copy.start()
+        raw_copies.append(copy)
+    rawr[piece(me)] = raws[piece(me)]
+
+    for copy in bc_copies:
+        copy.wait_recv()
+    b_pack = mm(p_recv, bcr[0]).astype(bf)
+    c_pack = mm(p_recv, bcr[1]).astype(bf)
+    b_turn = nt(eye(state), b_pack).astype(bf)
+    c_turn = nt(eye(state), c_pack).astype(bf)
+    gram = nt(c_pack, b_pack)
+    gram_t = nt(b_pack, c_pack)
+    for copy in x_copies:
+        copy.wait_recv()
+    xp[...] = mm(p_recv, xr[...]).astype(bf)
+    head_row, head_column = iotas(heads, width)
+    spread = one_hot(
+        (head_column >= head_row * head_dim) & (head_column < (head_row + 1) * head_dim)
+    )
+
+    def expand(array):
+        high, low = two_parts(array)
+        return mm(high, spread) + mm(low, spread)
+
+    for copy in raw_copies:
+        copy.wait_recv()
+    raw_step = mm(p_recv, rawr[...])
+    rate = jnp.exp(log_ref[...])
+    step = jnp.maximum(raw_step, 0.0) + jnp.log1p(jnp.exp(-jnp.abs(raw_step)))
+    log_decay = -step * rate
+    cumul = jnp.dot(
+        lower.astype(f32), log_decay, precision=HIGHEST_PRECISION, preferred_element_type=f32
+    )
+    total = cumul[length - 1 : length]
+    decay_total = jnp.exp(total) * alive_last
+    decay_wide = expand(jnp.broadcast_to(decay_total, (8, heads)))[0:1]
+    step_wide[...] = expand(step)
+    enter_wide[...] = expand(jnp.exp(cumul) * alive)
+    leave_wide[...] = expand(jnp.exp(total - cumul) * tail)
+    eg[...] = (enter_wide[...] * g_ref[...].astype(f32)).astype(bf)
+    lx[...] = (leave_wide[...] * step_wide[...] * xp[...].astype(f32)).astype(bf)
+
+    def lanes(c):
+        return slice(c * wide, (c + 1) * wide)
+
+    f_copies = [
+        remote(f_out.at[c], f_in.at[c], f_s.at[c], f_r.at[c], ctx=lax.rem(me + 1, n), dp=mine)
+        for c in range(chunks)
+    ]
+    b_copies = [
+        remote(g_out.at[c], g_in.at[c], b_s.at[c], b_r.at[c], ctx=lax.rem(me + n - 1, n), dp=mine)
+        for c in range(chunks)
+    ]
+    for c in range(chunks):
+        end_own[c] = mm(b_turn, lx[:, lanes(c)])
+
+        @pl.when(me == 0)
+        def _():
+            f_in[c] = jnp.zeros((state, wide), f_in.dtype)
+            f_out[c] = end_own[c].astype(f_out.dtype)
+            f_copies[c].start()
+
+        back_own[c] = mm(c_turn, eg[:, lanes(c)])
+
+        @pl.when(me == n - 1)
+        def _():
+            g_in[c] = jnp.zeros((state, wide), g_in.dtype)
+            g_out[c] = back_own[c].astype(g_out.dtype)
+            b_copies[c].start()
+
+    eye_f = eye(heads, f32)
+    cum_row[...] = nt(eye_f, cumul, HIGHEST_PRECISION)
+    step_row[...] = nt(eye_f, step, HIGHEST_PRECISION)
+    for k in range(heads // per):
+        cum_col[k, :, 0:per] = cumul[:, k * per : (k + 1) * per]
+    gram_grad[...] = jnp.zeros_like(gram_grad)
+    lane_head = lax.broadcasted_iota(jnp.int32, (length, 128), 1)
+
+    def only(array, q):
+        return jnp.where(
+            (lane_head >= q * head_dim) & (lane_head < (q + 1) * head_dim), array, 0.0
+        ).astype(bf)
+
+    def intra(at, _):
+        here = pl.ds(pl.multiple_of(at * 128, 128), 128)
+        g4 = g_ref[:, here].astype(f32)
+        x4 = xp[:, here].astype(f32)
+        s4 = x4 * step_wide[:, here]
+        stack = lambda array: jnp.concatenate([only(array, q) for q in range(per)], axis=0)
+        inner = nt(g4.astype(bf), stack(x4))
+        weights, turned = [], []
+        columns = cum_col[at]
+        grown = gram_grad[...]
+        for q in range(per):
+            across = cum_row[pl.ds(at * per + q, 1), :]
+            down = columns[:, q : q + 1]
+            apart = down - across
+            kernel = jnp.where(joined, jnp.exp(apart), 0.0)
+            kernel_t = jnp.where(joined_t, jnp.exp(-apart), 0.0)
+            scale = step_row[pl.ds(at * per + q, 1), :]
+            grown = grown + kernel * (inner[:, q * length : (q + 1) * length] * scale)
+            weights.append((kernel * gram).astype(bf))
+            turned.append((kernel_t * gram_t).astype(bf))
+        gram_grad[...] = grown
+        y_acc[:, here] = mm(jnp.concatenate(weights, axis=1), stack(s4))
+        gs_acc[:, here] = mm(jnp.concatenate(turned, axis=1), stack(g4))
+        return 0
+
+    grad_c = jnp.zeros((length, state), f32)
+    grad_b = jnp.zeros((length, state), f32)
+    out_sum = jnp.zeros((length, heads), f32)
+    in_sum = jnp.zeros((length, heads), f32)
+    last_extra = jnp.zeros((8, heads), f32)
+    groups = heads // per // chunks
+    for c in range(chunks):
+        lax.fori_loop(c * groups, (c + 1) * groups, intra, 0)
+
+        @pl.when(me > 0)
+        def _():
+            f_copies[c].wait_recv()
+
+        end_all[c] = decay_wide[:, lanes(c)] * f_in[c].astype(f32) + end_own[c]
+
+        @pl.when((me > 0) & (me < n - 1))
+        def _():
+            f_out[c] = end_all[c].astype(f_out.dtype)
+            f_copies[c].start()
+
+        @pl.when(me < n - 1)
+        def _():
+            b_copies[c].wait_recv()
+
+        @pl.when((me > 0) & (me < n - 1))
+        def _():
+            g_out[c] = (
+                decay_wide[:, lanes(c)] * g_in[c].astype(f32) + back_own[c]
+            ).astype(g_out.dtype)
+            b_copies[c].start()
+
+        state_in, state_grad = f_in[c].astype(bf), g_in[c].astype(bf)
+        y = y_acc[:, lanes(c)] + enter_wide[:, lanes(c)] * mm(c_pack, state_in)
+        grad_scaled = gs_acc[:, lanes(c)] + leave_wide[:, lanes(c)] * mm(b_pack, state_grad)
+        dx_ref[:, lanes(c)] = (grad_scaled * step_wide[:, lanes(c)]).astype(bf)
+        members = spread[:, lanes(c)]
+
+        def head_sum(array):
+            high, low = two_parts(array)
+            return nt(high, members) + nt(low, members)
+
+        out_sum = out_sum + head_sum(g_ref[:, lanes(c)].astype(f32) * y)
+        in_sum = in_sum + head_sum(xp[:, lanes(c)].astype(f32) * grad_scaled)
+        met = jnp.sum(g_in[c].astype(f32) * end_all[c], axis=0, keepdims=True)
+        last_extra = last_extra + head_sum(jnp.broadcast_to(met, (8, wide)))
+        grad_c = grad_c + nt(eg[:, lanes(c)], state_in)
+        grad_b = grad_b + nt(lx[:, lanes(c)], state_grad)
+
+    grad_cumul = out_sum - step * in_sum
+    grad_log = (
+        jnp.dot(
+            one_hot(row <= column, f32),
+            grad_cumul,
+            precision=HIGHEST_PRECISION,
+            preferred_element_type=f32,
+        )
+        + last_extra[0:1]
+    )
+    grad_raw = (in_sum - rate * grad_log) / (1.0 + jnp.exp(-raw_step))
+    gsl[...] = mm(p_back, grad_raw.astype(bf)).astype(bf)
+    gall[mine, piece(me)] = gsl[piece(me)]
+    g_copies = []
+    for kz in range(n):
+        for kd in range(m):
+            if kz or kd:
+                to = z_peer(kz)
+                copy = remote(
+                    gsl.at[piece(to)], gall.at[mine, piece(me)], g_s.at[kz, kd], g_r.at[kz, kd],
+                    ctx=to, dp=d_peer(kd),
+                )
+                copy.start()
+                g_copies.append(copy)
+
+    gram_b = gram_grad[...].astype(bf)
+    dc_ref[...] = grad_c + mm(gram_b, b_pack)
+    db_ref[...] = grad_b + mm(nt(eye(length), gram_b).astype(bf), c_pack)
+
+    for copy in u_copies:
+        copy.wait_recv()
+    for copy in g_copies:
+        copy.wait_recv()
+    eye_b = eye(heads)
+    turned_grads = [nt(eye_b, gall[d]).astype(bf) for d in range(m)]
+
+    def weight_part(z):
+        part = jnp.zeros((heads, block), f32)
+        for d in range(m):
+            part = part + mm(
+                turned_grads[d],
+                uall[d, :, pl.ds(pl.multiple_of(z * block, block), block)],
+            )
+        return part
+
+    p_copies = []
+    for k in range(1, n):
+        to = z_peer(k)
+        ps[k] = weight_part(to).astype(ps.dtype)
+        copy = remote(ps.at[k], pr.at[k], p_s.at[k], p_r.at[k], ctx=to, dp=mine)
+        copy.start()
+        p_copies.append(copy)
+    summed = weight_part(me)
+    for k, copy in enumerate(p_copies):
+        copy.wait_recv()
+        summed = summed + pr[k + 1].astype(f32)
+    dw_ref[...] = nt(eye(block, f32), summed, HIGHEST_PRECISION)
+
+    for copy in w_z + w_d + u_copies + x_copies + bc_copies + raw_copies + g_copies + p_copies:
+        copy.wait_send()
+    for c in range(chunks):
+
+        @pl.when(me < n - 1)
+        def _():
+            f_copies[c].wait_send()
+
+        @pl.when(me > 0)
+        def _():
+            b_copies[c].wait_send()
+
+
+def fits(n, m, rows_dev, length, heads, head_dim, state, block):
+    return (
+        rows_dev == 1
+        and length == 128
+        and (length // n) % 16 == 0
+        and 128 % head_dim == 0
+        and heads * head_dim % 512 == 0
+        and heads % 8 == 0
+        and block % 128 == 0
+    )
+
+
+def on_device_fused(
+    layer_input,
+    head_input,
+    input_map,
+    output_map,
+    step_weight,
+    decay_log,
+    pack_place,
+    doc_starts,
+    out_grad,
+):
+    n, m = lax.axis_size("ctx"), lax.axis_size("dp")
+    _, length, width = head_input.shape
+    heads, state, model = decay_log.shape[0], input_map.shape[2], layer_input.shape[2]
+    block = step_weight.shape[0]
+    chunks = 4
+    wide = width // chunks
+    per = 128 // (width // heads)
+    f32, bf = jnp.float32, jnp.bfloat16
+    dims = (n, m, length, heads, width // heads, state, chunks)
+    vmem, dma = pltpu.VMEM, pltpu.SemaphoreType.DMA
+    whole = pl.BlockSpec(memory_space=pltpu.VMEM)
+    scratch = [
+        vmem((m, n, heads, block), bf),
+        vmem((m, length, n * block), bf),
+        vmem((m, length, n * block), bf),
+        vmem((length, width), bf),
+        vmem((length, width), bf),
+        vmem((2, length, state), bf),
+        vmem((2, length, state), bf),
+        vmem((length, heads), bf),
+        vmem((length, heads), bf),
+        vmem((length, width), bf),
+        vmem((length, width), f32),
+        vmem((length, width), f32),
+        vmem((length, width), f32),
+        vmem((length, width), f32),
+        vmem((length, width), f32),
+        vmem((length, width), bf),
+        vmem((length, width), bf),
+        vmem((chunks, state, wide), f32),
+        vmem((chunks, state, wide), f32),
+        vmem((chunks, state, wide), f32),
+        vmem((chunks, state, wide), bf),
+        vmem((chunks, state, wide), bf),
+        vmem((chunks, state, wide), bf),
+        vmem((chunks, state, wide), bf),
+        vmem((heads // per, length, 128), f32),
+        vmem((heads, length), f32),
+        vmem((heads, length), f32),
+        vmem((length, length), f32),
+        vmem((length, heads), bf),
+        vmem((m, length, heads), bf),
+        vmem((n, heads, block), bf),
+        vmem((n, heads, block), bf),
+        dma((n,)), dma((n,)), dma((m,)), dma((m,)), dma((m,)), dma((m,)),
+        dma((n,)), dma((n,)), dma((n,)), dma((n,)), dma((n,)), dma((n,)),
+        dma((chunks,)), dma((chunks,)), dma((chunks,)), dma((chunks,)),
+        dma((n, m)), dma((n, m)), dma((n,)), dma((n,)),
+    ]
+    head_grad, grad_b, grad_c, weight_grad = pl.pallas_call(
+        functools.partial(layer_kernel, dims),
+        out_shape=(
+            jax.ShapeDtypeStruct((length, width), bf),
+            jax.ShapeDtypeStruct((length, state), f32),
+            jax.ShapeDtypeStruct((length, state), f32),
+            jax.ShapeDtypeStruct((block, heads), f32),
+        ),
+        in_specs=[whole] * 9,
+        out_specs=(whole,) * 4,
+        scratch_shapes=scratch,
+        compiler_params=pltpu.CompilerParams(
+            collective_id=0, has_side_effects=True, vmem_limit_bytes=48 * 1024 * 1024
+        ),
+    )(
+        layer_input[0],
+        head_input[0],
+        input_map[0],
+        output_map[0],
+        step_weight,
+        decay_log[None],
+        pack_place,
+        doc_starts,
+        out_grad[0],
+    )
+    return head_grad[None], grad_b[None], grad_c[None], weight_grad
+
+
 def solution(mesh):
     placed = (
         P(("groups", "dp"), "ctx", None),
@@ -183,8 +700,16 @@
         P(("groups", "dp"), "ctx"),
         P(("groups", "dp"), "ctx", None),
     )
+
+    def chosen(*arrays):
+        n, m = mesh.shape["ctx"], mesh.shape["dp"]
+        rows_dev, length, width = arrays[1].shape
+        heads = arrays[5].shape[0]
+        sizes = (rows_dev, length, heads, width // heads, arrays[2].shape[2], arrays[4].shape[0])
+        return (on_device_fused if fits(n, m, *sizes) else on_device)(*arrays)
+
     return jax.shard_map(
-        on_device,
+        chosen,
         mesh=mesh,
         in_specs=placed,
         out_specs=(

time: 342 us -> 87 us (0.25)
  waiting for transfers between devices: 165 us -> 0 us
  Pallas kernels: 0 us -> 77.4 us
  blocking collectives: 42.9 us -> 0 us
  matrix products: 37.1 us -> 0 us
  other arithmetic: 31.9 us -> 0 us
  local copies, waits for them, and re-layouts: 29.9 us -> 8.47 us
  starting transfers between devices: 17.5 us -> 0 us
  between operations: 15.2 us -> 0.68 us
    all_gather x2 -> x0, waiting for transfers between devices: 101 us -> none  [carried_in(): everything = jax.tree.map(lambda part: lax.all_gather(part, axis), array)]
    pallas_call x0 -> x1, Pallas kernels: none -> 77.4 us  [on_device_fused(): pl.pallas_call(functools.partial(layer_kernel, dims), out_shape=(jax.Shap...]
    reduce_scatter x1 -> x0, waiting for transfers between devices: 43.6 us -> none  [on_device(): lax.psum_scatter(lax.dot_general(columns, grad_flat, (((0,), (0,)), ((),...]
    all_gather x2 -> x0, blocking collectives: 42.9 us -> none  [the longest x1 24.8 us: on_device(): lax.all_gather(step_weight, ('ctx', 'dp'), axis=0, tiled=True)]
    dot_general x13 -> x0, matrix products: 37.1 us -> none  [the longest x11 34.4 us: contract(): return jnp.einsum(form, *operands, precision=HIGHEST_PRECISION)]
    all_to_all x5 -> x0, waiting for transfers between devices: 20.5 us -> none  [the longest x1 4.97 us: on_device(): lax.all_to_all(arranged, 'ctx', split_axis=1, concat_axis=1, tiled=True)]
    all_to_all x5 -> x0, starting transfers between devices: 17.4 us -> none  [the longest x1 4.35 us: on_device(): lax.all_to_all(for_sending(head_input), 'ctx', split_axis=1, concat_axis=...]
    select_n x12 -> x0, other arithmetic: 13.6 us -> none  [the longest x8 11.9 us: turn(): return jax.tree.map(lambda a, b: jnp.where(reached, a, b), new, before)]
  transfers between devices with their start and end apart: 8 -> 0, of which waited for: 8 -> 0; matrix products, arithmetic and copies ran while one was open for 14% -> 0% of each run, Pallas kernels for 0% -> 0%
where the time goes in v1:
time: 87 us; the launch traced here: 86.6 us
  Pallas kernels  77.4 us (89%)
  local copies, waits for them, and re-layouts  8.47 us (10%)
    pallas_call x1, Pallas kernels, on_device_fused(): pl.pallas_call(functools.partial(layer_kernel, dims), out_shape=(jax.Shap...  77.4 us
    unnamed x23, local copies, waits for them, and re-layouts  8.47 us

profile of v1, /device:TPU:0, one launch (start us, length us, event | category | flops | bytes accessed | tf_op | source)
XLA Modules:
  0.0 86.6 jit_solution(13924659451699462944)
XLA Ops:
  0.6 0.0 copy-start.7
  0.6 0.8 copy.13
  1.5 0.0 copy-start.6
  1.5 0.0 copy-done.7
  1.5 0.1 copy.14
  1.6 0.6 copy-done.6
  2.2 0.0 copy-start.3
  2.2 0.0 copy-start.4
  2.2 0.0 copy-start.5
  2.2 0.1 copy.15.w_ref
  2.4 0.6 copy-done.3
  2.9 0.0 copy-done.4
  2.9 0.0 copy-done.5
  2.9 0.0 copy-start
  2.9 1.2 %copy-done = bf16[1,128,4096]{2,1,0:T(8,128)(2,1)S(1)} copy-done((bf16[1,128,4096]{2,1,0:T(8,128)(2,1)S(1)}, bf16[1,128,4096]{2,1,0:T(8,128)(2,1)}, u32[]{:S(2)}) %copy-start) | copy-done | bytes 1048600
  4.2 0.0 copy-start.1
  4.2 1.0 %copy-done.1 = bf16[1,128,2048]{2,1,0:T(8,128)(2,1)S(1)} copy-done((bf16[1,128,2048]{2,1,0:T(8,128)(2,1)S(1)}, bf16[1,128,2048]{2,1,0:T(8,128)(2,1)}, u32[]{:S(2)}) %copy-start.1) | copy-done | bytes 524312
  5.2 0.0 copy-start.2
  5.2 1.0 %copy-done.2 = bf16[1,128,2048]{2,1,0:T(8,128)(2,1)S(1)} copy-done((bf16[1,128,2048]{2,1,0:T(8,128)(2,1)S(1)}, bf16[1,128,2048]{2,1,0:T(8,128)(2,1)}, u32[]{:S(2)}) %copy-start.2) | copy-done | bytes 524312
  6.2 77.4 %shard_map.120 = (bf16[128,2048]{1,0:T(8,128)(2,1)S(1)}, f32[128,64]{1,0:T(8,128)S(1)}, f32[128,64]{1,0:T(8,128)S(1)}, f32[256,64]{1,0:T(8,128)S(1)}) custom-call(bf16[128,4096]{1,0:T(8,128)(2,1)S(1)} %bitcast.9, bf16[128,2048]{1,0:T(8,128)(2,1)S(1)} %bitcast.10, bf16[128,64]{1,0:T(8,128)(2,1)S(1)} %bitcast.13, bf16[128,64]{1,0:T(8,128)(2,1)S(1)} %bitcast.14, ...), custom_call_target="tpu_custom_call" | custom-call | tf_op jit(solution)/shard_map/pallas_call | solution.py:663
  83.7 0.7 copy.16
  84.4 0.7 copy.17
  85.1 0.7 copy.18
  85.8 0.8 copy.20
Async XLA Ops:
  0.6 0.9 copy-start.7
  1.5 0.8 copy-start.6
  2.2 0.7 copy-start.3
  2.2 0.7 copy-start.4
  2.2 0.7 copy-start.5
  2.9 1.2 %copy-start = (bf16[1,128,4096]{2,1,0:T(8,128)(2,1)S(1)}, bf16[1,128,4096]{2,1,0:T(8,128)(2,1)}, u32[]{:S(2)}) copy-start(bf16[1,128,4096]{2,1,0:T(8,128)(2,1)} %param.9) | copy-start | bytes 3145732
  4.2 1.0 %copy-start.1 = (bf16[1,128,2048]{2,1,0:T(8,128)(2,1)S(1)}, bf16[1,128,2048]{2,1,0:T(8,128)(2,1)}, u32[]{:S(2)}) copy-start(bf16[1,128,2048]{2,1,0:T(8,128)(2,1)} %param.10) | copy-start | bytes 1572868
  5.2 1.0 %copy-start.2 = (bf16[1,128,2048]{2,1,0:T(8,128)(2,1)S(1)}, bf16[1,128,2048]{2,1,0:T(8,128)(2,1)}, u32[]{:S(2)}) copy-start(bf16[1,128,2048]{2,1,0:T(8,128)(2,1)} %param.17) | copy-start | bytes 1572868

commit v2 on v1

--- a/solution.py
+++ b/solution.py
@@ -219,20 +219,21 @@
 
 def layer_kernel(
     dims,
-    u_ref, x_ref, b_ref, c_ref, w_ref, log_ref, place_ref, start_ref, g_ref,
+    u_hbm, x_hbm, b_hbm, c_hbm, w_hbm, log_hbm, place_hbm, start_hbm, g_hbm,
     dx_ref, db_ref, dc_ref, dw_ref,
+    u_ref, x_ref, bc_ref, log_ref, place_ref, start_ref, g_ref,
     wall, us, uall, xs, xr, bcs, bcr, raws, rawr, xp,
     step_wide, enter_wide, leave_wide, y_acc, gs_acc, eg, lx,
-    end_own, back_own, end_all, f_out, f_in, g_out, g_in,
+    end_own, back_own, f_out, f_in, g_out, g_in,
     cum_col, cum_row, step_row, gram_grad, gsl, gall, ps, pr,
     wz_s, wz_r, wd_s, wd_r, u_s, u_r, x_s, x_r, bc_s, bc_r, raw_s, raw_r,
-    f_s, f_r, b_s, b_r, g_s, g_r, p_s, p_r,
+    f_s, f_r, b_s, b_r, g_s, g_r, p_s, p_r, in_s,
 ):
     n, m, length, heads, head_dim, state, chunks = dims
     f32, bf = jnp.float32, jnp.bfloat16
     me, mine = lax.axis_index("ctx"), lax.axis_index("dp")
     rows = length // n
-    block = w_ref.shape[0]
+    block = w_hbm.shape[1]
     width = heads * head_dim
     wide = width // chunks
     per = 128 // head_dim
@@ -255,7 +256,24 @@
                     device_id_type=pl.DeviceIdType.MESH,
                 )
 
-    wall[mine, me] = nt(eye(heads), w_ref[...]).astype(bf)
+    loads = [
+        pltpu.make_async_copy(src, dst, in_s.at[k])
+        for k, (src, dst) in enumerate(
+            (
+                (place_hbm, place_ref),
+                (w_hbm, wall.at[mine, me]),
+                (x_hbm, x_ref),
+                (b_hbm, bc_ref.at[0:state]),
+                (c_hbm, bc_ref.at[state : 2 * state]),
+                (u_hbm, u_ref),
+                (start_hbm, start_ref),
+                (log_hbm, log_ref),
+                (g_hbm, g_ref),
+            )
+        )
+    ]
+    for load in loads:
+        load.start()
     row, column = iotas(length, length)
     row_f = row.astype(f32)
     before = one_hot(row < column)
@@ -264,6 +282,7 @@
     def prefix(flags):
         return mm(jnp.broadcast_to(flags, (8, length)).astype(bf), before)[0:1]
 
+    loads[0].wait()
     own_place = jnp.zeros((1, length), jnp.int32)
     for k in range(n):
         own_place = jnp.where(me == k, place_ref[:, k * length : (k + 1) * length], own_place)
@@ -272,6 +291,7 @@
         flags = one_hot((own_place >= k * length) & (own_place < (k + 1) * length), f32)
         slot = slot + flags * (k * rows + prefix(flags))
     p_send = one_hot(slot == row_f)
+    loads[1].wait()
     pl.semaphore_wait(barrier, n * m - 1)
 
     w_z = []
@@ -282,25 +302,10 @@
         copy.start()
         w_z.append(copy)
 
+    for load in loads[2:6]:
+        load.wait()
     xs[...] = mm(p_send, x_ref[...]).astype(bf)
-    bcs[0] = mm(p_send, b_ref[...]).astype(bf)
-    bcs[1] = mm(p_send, c_ref[...]).astype(bf)
-    x_copies, bc_copies = [], []
-    for k in range(1, n):
-        to = z_peer(k)
-        copy = remote(
-            bcs.at[:, piece(to)], bcr.at[:, piece(me)], bc_s.at[k], bc_r.at[k], ctx=to, dp=mine
-        )
-        copy.start()
-        bc_copies.append(copy)
-    for k in range(1, n):
-        to = z_peer(k)
-        copy = remote(xs.at[piece(to)], xr.at[piece(me)], x_s.at[k], x_r.at[k], ctx=to, dp=mine)
-        copy.start()
-        x_copies.append(copy)
-    bcr[:, piece(me)] = bcs[:, piece(me)]
-    xr[piece(me)] = xs[piece(me)]
-
+    bcs[...] = nt(p_send, bc_ref[...]).astype(bf)
     for copy in w_z:
         copy.wait_recv()
     w_d = []
@@ -310,6 +315,21 @@
         )
         copy.start()
         w_d.append(copy)
+    x_copies, bc_copies = [], []
+    for k in range(1, n):
+        to = z_peer(k)
+        copy = remote(
+            bcs.at[piece(to)], bcr.at[piece(me)], bc_s.at[k], bc_r.at[k], ctx=to, dp=mine
+        )
+        copy.start()
+        bc_copies.append(copy)
+    for k in range(1, n):
+        to = z_peer(k)
+        copy = remote(xs.at[piece(to)], xr.at[piece(me)], x_s.at[k], x_r.at[k], ctx=to, dp=mine)
+        copy.start()
+        x_copies.append(copy)
+    bcr[piece(me)] = bcs[piece(me)]
+    xr[piece(me)] = xs[piece(me)]
 
     for d in range(m):
         for z in range(n):
@@ -317,12 +337,6 @@
             us[d, :, z * block : (z + 1) * block] = mm(
                 p_send, u_ref[:, at : at + block]
             ).astype(bf)
-    u_copies = []
-    for k in range(1, m):
-        to = d_peer(k)
-        copy = remote(us.at[to], uall.at[mine], u_s.at[k], u_r.at[k], ctx=me, dp=to)
-        copy.start()
-        u_copies.append(copy)
     uall[mine] = us[mine]
 
     p_recv = jnp.zeros((length, length), f32)
@@ -337,6 +351,8 @@
         p_back = p_back + nt(comes, lands)
     p_recv, p_back = p_recv.astype(bf), p_back.astype(bf)
 
+    for load in loads[6:]:
+        load.wait()
     starts = jnp.broadcast_to(start_ref[...].astype(f32), (8, length)).astype(bf)
     seg_col = nt(lower, starts)[:, 0:1]
     seg_row = nt(starts, lower)[0:1]
@@ -364,13 +380,19 @@
         copy.start()
         raw_copies.append(copy)
     rawr[piece(me)] = raws[piece(me)]
+    u_copies = []
+    for k in range(1, m):
+        to = d_peer(k)
+        copy = remote(us.at[to], uall.at[mine], u_s.at[k], u_r.at[k], ctx=me, dp=to)
+        copy.start()
+        u_copies.append(copy)
 
     for copy in bc_copies:
         copy.wait_recv()
-    b_pack = mm(p_recv, bcr[0]).astype(bf)
-    c_pack = mm(p_recv, bcr[1]).astype(bf)
-    b_turn = nt(eye(state), b_pack).astype(bf)
-    c_turn = nt(eye(state), c_pack).astype(bf)
+    both = mm(p_recv, bcr[...]).astype(bf)
+    b_pack, c_pack = both[:, :state], both[:, state:]
+    both_turned = nt(eye(2 * state), both).astype(bf)
+    b_turn, c_turn = both_turned[:state], both_turned[state:]
     gram = nt(c_pack, b_pack)
     gram_t = nt(b_pack, c_pack)
     for copy in x_copies:
@@ -469,26 +491,26 @@
         gs_acc[:, here] = mm(jnp.concatenate(turned, axis=1), stack(g4))
         return 0
 
-    grad_c = jnp.zeros((length, state), f32)
-    grad_b = jnp.zeros((length, state), f32)
+    grad_c = jnp.zeros((state, length), f32)
+    grad_b = jnp.zeros((state, length), f32)
     out_sum = jnp.zeros((length, heads), f32)
     in_sum = jnp.zeros((length, heads), f32)
     last_extra = jnp.zeros((8, heads), f32)
     groups = heads // per // chunks
-    for c in range(chunks):
-        lax.fori_loop(c * groups, (c + 1) * groups, intra, 0)
-
+
+    def relay_forward(c):
         @pl.when(me > 0)
         def _():
             f_copies[c].wait_recv()
 
-        end_all[c] = decay_wide[:, lanes(c)] * f_in[c].astype(f32) + end_own[c]
-
         @pl.when((me > 0) & (me < n - 1))
         def _():
-            f_out[c] = end_all[c].astype(f_out.dtype)
+            f_out[c] = (
+                decay_wide[:, lanes(c)] * f_in[c].astype(f32) + end_own[c]
+            ).astype(f_out.dtype)
             f_copies[c].start()
 
+    def relay_back(c):
         @pl.when(me < n - 1)
         def _():
             b_copies[c].wait_recv()
@@ -500,6 +522,28 @@
             ).astype(g_out.dtype)
             b_copies[c].start()
 
+    for c in range(chunks):
+        lax.fori_loop(c * groups, (c + 1) * groups, intra, 0)
+
+        @pl.when(me < n // 2)
+        def _():
+            relay_forward(c)
+
+        @pl.when(me >= n // 2)
+        def _():
+            relay_back(c)
+
+    for c in range(chunks):
+
+        @pl.when(me < n // 2)
+        def _():
+            relay_back(c)
+
+        @pl.when(me >= n // 2)
+        def _():
+            relay_forward(c)
+
+        end_all = decay_wide[:, lanes(c)] * f_in[c].astype(f32) + end_own[c]
         state_in, state_grad = f_in[c].astype(bf), g_in[c].astype(bf)
         y = y_acc[:, lanes(c)] + enter_wide[:, lanes(c)] * mm(c_pack, state_in)
         grad_scaled = gs_acc[:, lanes(c)] + leave_wide[:, lanes(c)] * mm(b_pack, state_grad)
@@ -512,10 +556,10 @@
 
         out_sum = out_sum + head_sum(g_ref[:, lanes(c)].astype(f32) * y)
         in_sum = in_sum + head_sum(xp[:, lanes(c)].astype(f32) * grad_scaled)
-        met = jnp.sum(g_in[c].astype(f32) * end_all[c], axis=0, keepdims=True)
+        met = jnp.sum(g_in[c].astype(f32) * end_all, axis=0, keepdims=True)
         last_extra = last_extra + head_sum(jnp.broadcast_to(met, (8, wide)))
-        grad_c = grad_c + nt(eg[:, lanes(c)], state_in)
-        grad_b = grad_b + nt(lx[:, lanes(c)], state_grad)
+        grad_c = grad_c + nt(state_in, eg[:, lanes(c)])
+        grad_b = grad_b + nt(state_grad, lx[:, lanes(c)])
 
     grad_cumul = out_sum - step * in_sum
     grad_log = (
@@ -528,7 +572,7 @@
         + last_extra[0:1]
     )
     grad_raw = (in_sum - rate * grad_log) / (1.0 + jnp.exp(-raw_step))
-    gsl[...] = mm(p_back, grad_raw.astype(bf)).astype(bf)
+    gsl[...] = mm(p_back, jnp.concatenate(two_parts(grad_raw), axis=1)).astype(bf)
     gall[mine, piece(me)] = gsl[piece(me)]
     g_copies = []
     for kz in range(n):
@@ -543,24 +587,24 @@
                 g_copies.append(copy)
 
     gram_b = gram_grad[...].astype(bf)
-    dc_ref[...] = grad_c + mm(gram_b, b_pack)
-    db_ref[...] = grad_b + mm(nt(eye(length), gram_b).astype(bf), c_pack)
+    dc_ref[...] = grad_c + nt(b_turn, gram_b)
+    db_ref[...] = grad_b + mm(c_turn, gram_b)
 
     for copy in u_copies:
         copy.wait_recv()
     for copy in g_copies:
         copy.wait_recv()
-    eye_b = eye(heads)
+    eye_b = eye(2 * heads)
     turned_grads = [nt(eye_b, gall[d]).astype(bf) for d in range(m)]
 
     def weight_part(z):
-        part = jnp.zeros((heads, block), f32)
+        part = jnp.zeros((2 * heads, block), f32)
         for d in range(m):
             part = part + mm(
                 turned_grads[d],
                 uall[d, :, pl.ds(pl.multiple_of(z * block, block), block)],
             )
-        return part
+        return part[:heads] + part[heads:]
 
     p_copies = []
     for k in range(1, n):
@@ -573,7 +617,7 @@
     for k, copy in enumerate(p_copies):
         copy.wait_recv()
         summed = summed + pr[k + 1].astype(f32)
-    dw_ref[...] = nt(eye(block, f32), summed, HIGHEST_PRECISION)
+    dw_ref[...] = summed
 
     for copy in w_z + w_d + u_copies + x_copies + bc_copies + raw_copies + g_copies + p_copies:
         copy.wait_send()
@@ -586,6 +630,12 @@
         @pl.when(me > 0)
         def _():
             b_copies[c].wait_send()
+
+
+def hand_over(*refs):
+    half = len(refs) // 2
+    for source, target in zip(refs[:half], refs[half:]):
+        target[...] = source[...]
 
 
 def fits(n, m, rows_dev, length, heads, head_dim, state, block):
@@ -623,13 +673,20 @@
     vmem, dma = pltpu.VMEM, pltpu.SemaphoreType.DMA
     whole = pl.BlockSpec(memory_space=pltpu.VMEM)
     scratch = [
+        vmem((length, n * m * block), bf),
+        vmem((length, width), bf),
+        vmem((2 * state, length), bf),
+        vmem((1, heads), f32),
+        vmem((1, n * length), jnp.int32),
+        vmem((1, length), jnp.int32),
+        vmem((length, width), bf),
         vmem((m, n, heads, block), bf),
         vmem((m, length, n * block), bf),
         vmem((m, length, n * block), bf),
         vmem((length, width), bf),
         vmem((length, width), bf),
-        vmem((2, length, state), bf),
-        vmem((2, length, state), bf),
+        vmem((length, 2 * state), bf),
+        vmem((length, 2 * state), bf),
         vmem((length, heads), bf),
         vmem((length, heads), bf),
         vmem((length, width), bf),
@@ -642,7 +699,6 @@
         vmem((length, width), bf),
         vmem((chunks, state, wide), f32),
         vmem((chunks, state, wide), f32),
-        vmem((chunks, state, wide), f32),
         vmem((chunks, state, wide), bf),
         vmem((chunks, state, wide), bf),
         vmem((chunks, state, wide), bf),
@@ -651,41 +707,45 @@
         vmem((heads, length), f32),
         vmem((heads, length), f32),
         vmem((length, length), f32),
-        vmem((length, heads), bf),
-        vmem((m, length, heads), bf),
+        vmem((length, 2 * heads), bf),
+        vmem((m, length, 2 * heads), bf),
         vmem((n, heads, block), bf),
         vmem((n, heads, block), bf),
         dma((n,)), dma((n,)), dma((m,)), dma((m,)), dma((m,)), dma((m,)),
         dma((n,)), dma((n,)), dma((n,)), dma((n,)), dma((n,)), dma((n,)),
         dma((chunks,)), dma((chunks,)), dma((chunks,)), dma((chunks,)),
-        dma((n, m)), dma((n, m)), dma((n,)), dma((n,)),
+        dma((n, m)), dma((n, m)), dma((n,)), dma((n,)), dma((9,)),
     ]
-    head_grad, grad_b, grad_c, weight_grad = pl.pallas_call(
+    results = (
+        jax.ShapeDtypeStruct((length, width), bf),
+        jax.ShapeDtypeStruct((state, length), f32),
+        jax.ShapeDtypeStruct((state, length), f32),
+        jax.ShapeDtypeStruct((heads, block), f32),
+    )
+    grads = pl.pallas_call(
         functools.partial(layer_kernel, dims),
-        out_shape=(
-            jax.ShapeDtypeStruct((length, width), bf),
-            jax.ShapeDtypeStruct((length, state), f32),
-            jax.ShapeDtypeStruct((length, state), f32),
-            jax.ShapeDtypeStruct((block, heads), f32),
-        ),
-        in_specs=[whole] * 9,
+        out_shape=results,
+        in_specs=[pl.BlockSpec(memory_space=pltpu.HBM)] * 9,
         out_specs=(whole,) * 4,
         scratch_shapes=scratch,
         compiler_params=pltpu.CompilerParams(
-            collective_id=0, has_side_effects=True, vmem_limit_bytes=48 * 1024 * 1024
+            collective_id=0, has_side_effects=True, vmem_limit_bytes=56 * 1024 * 1024
         ),
     )(
         layer_input[0],
         head_input[0],
-        input_map[0],
-        output_map[0],
-        step_weight,
+        input_map[0].T,
+        output_map[0].T,
+        step_weight.T,
         decay_log[None],
         pack_place,
         doc_starts,
         out_grad[0],
     )
-    return head_grad[None], grad_b[None], grad_c[None], weight_grad
+    head_grad, grad_b, grad_c, weight_grad = pl.pallas_call(
+        hand_over, out_shape=results, in_specs=[whole] * 4, out_specs=(whole,) * 4
+    )(*grads)
+    return head_grad[None], grad_b.T[None], grad_c.T[None], weight_grad.T
 
 
 def solution(mesh):

time: 87 us -> 57.2 us (0.66)
  Pallas kernels: 77.4 us -> 56.4 us
  local copies, waits for them, and re-layouts: 8.47 us -> 0 us
    pallas_call x1 -> x2, Pallas kernels: 77.4 us -> 56.4 us  [the longest x1 54.5 us: on_device_fused(): pl.pallas_call(functools.partial(layer_kernel, dims), out_shape=results,...]
    unnamed x23 -> x0, local copies, waits for them, and re-layouts: 8.47 us -> none
where the time goes in v2:
time: 57.2 us; the launch traced here: 57.1 us
  Pallas kernels  56.4 us (99%)
  between operations  0.64 us (1%)
    pallas_call x1, Pallas kernels, on_device_fused(): pl.pallas_call(functools.partial(layer_kernel, dims), out_shape=results,...  54.5 us
    pallas_call x1, Pallas kernels, on_device_fused(): pl.pallas_call(hand_over, out_shape=results, in_specs=[whole] * 4, out_sp...  1.92 us

profile of v2, /device:TPU:0, one launch (start us, length us, event | category | flops | bytes accessed | tf_op | source)
XLA Modules:
  0.0 57.1 jit_solution(16754986726230867436)
XLA Ops:
  0.6 54.5 %shard_map.120 = (bf16[128,2048]{1,0:T(8,128)(2,1)}, f32[64,128]{1,0:T(8,128)}, f32[64,128]{1,0:T(8,128)}, f32[64,256]{1,0:T(8,128)}) custom-call(bf16[128,4096]{1,0:T(8,128)(2,1)} %bitcast.19, bf16[128,2048]{1,0:T(8,128)(2,1)} %bitcast.20, bf16[64,128]{1,0:T(8,128)(2,1)} %bitcast.23, bf16[64,128]{1,0:T(8,128)(2,1)} %bitcast.24, bf16[64,256]{1,0:T(8,128)(2,1)} %bitcast.22, ...), custom_call_target="tpu_custom_call" | custom-call | tf_op jit(solution)/shard_map/pallas_call | solution.py:725
  55.1 1.9 %shard_map.121 = (bf16[128,2048]{1,0:T(8,128)(2,1)}, f32[64,128]{1,0:T(8,128)}, f32[64,128]{1,0:T(8,128)}, f32[64,256]{1,0:T(8,128)}) custom-call(bf16[128,2048]{1,0:T(8,128)(2,1)} %get-tuple-element.12.refs_0_, f32[64,128]{1,0:T(8,128)} %get-tuple-element.13.refs_1_, f32[64,128]{1,0:T(8,128)} %get-tuple-element.14.refs_2_, f32[64,256]{1,0:T(8,128)} %get-tuple-element.15.refs_3_), custom_call_target="tpu_custom_call" | custom-call | tf_op jit(solution)/shard_map/pallas_call | solution.py:745

commit v3 on v2

--- a/solution.py
+++ b/solution.py
@@ -226,7 +226,7 @@
     step_wide, enter_wide, leave_wide, y_acc, gs_acc, eg, lx,
     end_own, back_own, f_out, f_in, g_out, g_in,
     cum_col, cum_row, step_row, gram_grad, gsl, gall, ps, pr,
-    wz_s, wz_r, wd_s, wd_r, u_s, u_r, x_s, x_r, bc_s, bc_r, raw_s, raw_r,
+    wz_s, wz_r, wx_s, wx_r, wc_s, wc_r, u_s, u_r, x_s, x_r, bc_s, bc_r, raw_s, raw_r,
     f_s, f_r, b_s, b_r, g_s, g_r, p_s, p_r, in_s,
 ):
     n, m, length, heads, head_dim, state, chunks = dims
@@ -302,20 +302,50 @@
         copy.start()
         w_z.append(copy)
 
+    other = mine + 1 - 2 * lax.rem(mine, 2)
+    chips = m // 2
+    w_chip, w_core = [], []
+
+    def z_from(k):
+        return lax.rem(me + n - k, n)
+
+    def pass_on(j, k):
+        held = wall.at[lax.rem(mine + m - 2 * j, m), z_from(k)]
+        copy = remote(held, held, wc_s.at[j, k], wc_r.at[j, k], ctx=me, dp=other)
+        copy.start()
+        w_core.append(copy)
+
+    def spread_out(k):
+        for j in range(1, chips):
+            held = wall.at[mine, z_from(k)]
+            copy = remote(
+                held, held, wx_s.at[j, k], wx_r.at[j, k], ctx=me, dp=lax.rem(mine + 2 * j, m)
+            )
+            copy.start()
+            w_chip.append((j, k, copy))
+        pass_on(0, k)
+
+    spread_out(0)
     for load in loads[2:6]:
         load.wait()
-    xs[...] = mm(p_send, x_ref[...]).astype(bf)
     bcs[...] = nt(p_send, bc_ref[...]).astype(bf)
-    for copy in w_z:
-        copy.wait_recv()
-    w_d = []
-    for k in range(1, m):
-        copy = remote(
-            wall.at[mine], wall.at[mine], wd_s.at[k], wd_r.at[k], ctx=me, dp=d_peer(k)
-        )
-        copy.start()
-        w_d.append(copy)
-    x_copies, bc_copies = [], []
+    x_copies, bc_copies = [[] for _ in range(chunks)], []
+
+    def lanes(c):
+        return slice(c * wide, (c + 1) * wide)
+
+    def send_x(c):
+        xs[c] = mm(p_send, x_ref[:, lanes(c)]).astype(bf)
+        for k in range(1, n):
+            to = z_peer(k)
+            copy = remote(
+                xs.at[c, piece(to)], xr.at[c, piece(me)], x_s.at[c, k], x_r.at[c, k],
+                ctx=to, dp=mine,
+            )
+            copy.start()
+            x_copies[c].append(copy)
+        xr[c, piece(me)] = xs[c, piece(me)]
+
     for k in range(1, n):
         to = z_peer(k)
         copy = remote(
@@ -323,13 +353,8 @@
         )
         copy.start()
         bc_copies.append(copy)
-    for k in range(1, n):
-        to = z_peer(k)
-        copy = remote(xs.at[piece(to)], xr.at[piece(me)], x_s.at[k], x_r.at[k], ctx=to, dp=mine)
-        copy.start()
-        x_copies.append(copy)
+    send_x(0)
     bcr[piece(me)] = bcs[piece(me)]
-    xr[piece(me)] = xs[piece(me)]
 
     for d in range(m):
         for z in range(n):
@@ -363,13 +388,23 @@
     tail = one_hot(seg_col == seg_last, f32)
     alive_last = one_hot(seg_last == 0.0, f32)
 
+    for k in range(1, n):
+        w_z[k - 1].wait_recv()
+        spread_out(k)
+    for c in range(1, chunks // 2):
+        send_x(c)
+    for j, k, copy in w_chip:
+        copy.wait_recv()
+        pass_on(j, k)
     raw = jnp.zeros((length, heads), f32)
-    for k in range(m):
-        if k:
-            w_d[k - 1].wait_recv()
-        part = lax.rem(mine + m - k, m)
-        for z in range(n):
-            raw = raw + nt(us[part, :, z * block : (z + 1) * block], wall[part, z])
+    for core in range(2):
+        if core:
+            for copy in w_core:
+                copy.wait_recv()
+        for chip in range(chips):
+            part = lax.rem(jnp.where(core, other, mine) + 2 * chip, m)
+            for z in range(n):
+                raw = raw + nt(us[part, :, z * block : (z + 1) * block], wall[part, z])
     raws[...] = raw.astype(bf)
     raw_copies = []
     for k in range(1, n):
@@ -380,12 +415,8 @@
         copy.start()
         raw_copies.append(copy)
     rawr[piece(me)] = raws[piece(me)]
-    u_copies = []
-    for k in range(1, m):
-        to = d_peer(k)
-        copy = remote(us.at[to], uall.at[mine], u_s.at[k], u_r.at[k], ctx=me, dp=to)
-        copy.start()
-        u_copies.append(copy)
+    for c in range(chunks // 2, chunks):
+        send_x(c)
 
     for copy in bc_copies:
         copy.wait_recv()
@@ -395,9 +426,6 @@
     b_turn, c_turn = both_turned[:state], both_turned[state:]
     gram = nt(c_pack, b_pack)
     gram_t = nt(b_pack, c_pack)
-    for copy in x_copies:
-        copy.wait_recv()
-    xp[...] = mm(p_recv, xr[...]).astype(bf)
     head_row, head_column = iotas(heads, width)
     spread = one_hot(
         (head_column >= head_row * head_dim) & (head_column < (head_row + 1) * head_dim)
@@ -409,6 +437,12 @@
 
     for copy in raw_copies:
         copy.wait_recv()
+    u_copies = []
+    for k in range(1, m):
+        to = d_peer(k)
+        copy = remote(us.at[to], uall.at[mine], u_s.at[k], u_r.at[k], ctx=me, dp=to)
+        copy.start()
+        u_copies.append(copy)
     raw_step = mm(p_recv, rawr[...])
     rate = jnp.exp(log_ref[...])
     step = jnp.maximum(raw_step, 0.0) + jnp.log1p(jnp.exp(-jnp.abs(raw_step)))
@@ -423,10 +457,6 @@
     enter_wide[...] = expand(jnp.exp(cumul) * alive)
     leave_wide[...] = expand(jnp.exp(total - cumul) * tail)
     eg[...] = (enter_wide[...] * g_ref[...].astype(f32)).astype(bf)
-    lx[...] = (leave_wide[...] * step_wide[...] * xp[...].astype(f32)).astype(bf)
-
-    def lanes(c):
-        return slice(c * wide, (c + 1) * wide)
 
     f_copies = [
         remote(f_out.at[c], f_in.at[c], f_s.at[c], f_r.at[c], ctx=lax.rem(me + 1, n), dp=mine)
@@ -437,14 +467,6 @@
         for c in range(chunks)
     ]
     for c in range(chunks):
-        end_own[c] = mm(b_turn, lx[:, lanes(c)])
-
-        @pl.when(me == 0)
-        def _():
-            f_in[c] = jnp.zeros((state, wide), f_in.dtype)
-            f_out[c] = end_own[c].astype(f_out.dtype)
-            f_copies[c].start()
-
         back_own[c] = mm(c_turn, eg[:, lanes(c)])
 
         @pl.when(me == n - 1)
@@ -493,9 +515,7 @@
 
     grad_c = jnp.zeros((state, length), f32)
     grad_b = jnp.zeros((state, length), f32)
-    out_sum = jnp.zeros((length, heads), f32)
-    in_sum = jnp.zeros((length, heads), f32)
-    last_extra = jnp.zeros((8, heads), f32)
+    head_sums = jnp.zeros((3 * length + 32, heads), f32)
     groups = heads // per // chunks
 
     def relay_forward(c):
@@ -523,6 +543,20 @@
             b_copies[c].start()
 
     for c in range(chunks):
+        for copy in x_copies[c]:
+            copy.wait_recv()
+        xp[:, lanes(c)] = mm(p_recv, xr[c]).astype(bf)
+        lx[:, lanes(c)] = (
+            leave_wide[:, lanes(c)] * step_wide[:, lanes(c)] * xp[:, lanes(c)].astype(f32)
+        ).astype(bf)
+        end_own[c] = mm(b_turn, lx[:, lanes(c)])
+
+        @pl.when(me == 0)
+        def _():
+            f_in[c] = jnp.zeros((state, wide), f_in.dtype)
+            f_out[c] = end_own[c].astype(f_out.dtype)
+            f_copies[c].start()
+
         lax.fori_loop(c * groups, (c + 1) * groups, intra, 0)
 
         @pl.when(me < n // 2)
@@ -550,17 +584,19 @@
         dx_ref[:, lanes(c)] = (grad_scaled * step_wide[:, lanes(c)]).astype(bf)
         members = spread[:, lanes(c)]
 
-        def head_sum(array):
-            high, low = two_parts(array)
-            return nt(high, members) + nt(low, members)
-
-        out_sum = out_sum + head_sum(g_ref[:, lanes(c)].astype(f32) * y)
-        in_sum = in_sum + head_sum(xp[:, lanes(c)].astype(f32) * grad_scaled)
         met = jnp.sum(g_in[c].astype(f32) * end_all, axis=0, keepdims=True)
-        last_extra = last_extra + head_sum(jnp.broadcast_to(met, (8, wide)))
+        high, low = two_parts(xp[:, lanes(c)].astype(f32) * grad_scaled)
+        out_terms = (g_ref[:, lanes(c)].astype(f32) * y).astype(bf)
+        terms = (out_terms, high, low, *two_parts(jnp.broadcast_to(met, (16, wide))))
+        head_sums = head_sums + nt(jnp.concatenate(terms, axis=0), members)
         grad_c = grad_c + nt(state_in, eg[:, lanes(c)])
         grad_b = grad_b + nt(state_grad, lx[:, lanes(c)])
 
+    out_sum = head_sums[:length]
+    in_sum = head_sums[length : 2 * length] + head_sums[2 * length : 3 * length]
+    last_extra = head_sums[3 * length : 3 * length + 8] + head_sums[
+        3 * length + 16 : 3 * length + 24
+    ]
     grad_cumul = out_sum - step * in_sum
     grad_log = (
         jnp.dot(
@@ -619,7 +655,7 @@
         summed = summed + pr[k + 1].astype(f32)
     dw_ref[...] = summed
 
-    for copy in w_z + w_d + u_copies + x_copies + bc_copies + raw_copies + g_copies + p_copies:
+    for copy in w_z + [w[2] for w in w_chip] + w_core + u_copies + sum(x_copies, []) + bc_copies + raw_copies + g_copies + p_copies:
         copy.wait_send()
     for c in range(chunks):
 
@@ -633,9 +669,14 @@
 
 
 def hand_over(*refs):
-    half = len(refs) // 2
-    for source, target in zip(refs[:half], refs[half:]):
-        target[...] = source[...]
+    count = len(refs) // 2
+    copies = [
+        pltpu.make_async_copy(refs[k], refs[count + k], refs[-1].at[k]) for k in range(count)
+    ]
+    for copy in copies:
+        copy.start()
+    for copy in copies:
+        copy.wait()
 
 
 def fits(n, m, rows_dev, length, heads, head_dim, state, block):
@@ -644,9 +685,10 @@
         and length == 128
         and (length // n) % 16 == 0
         and 128 % head_dim == 0
-        and heads * head_dim % 512 == 0
+        and heads * head_dim % 1024 == 0
         and heads % 8 == 0
         and block % 128 == 0
+        and m % 2 == 0
     )
 
 
@@ -683,8 +725,8 @@
         vmem((m, n, heads, block), bf),
         vmem((m, length, n * block), bf),
         vmem((m, length, n * block), bf),
-        vmem((length, width), bf),
-        vmem((length, width), bf),
+        vmem((chunks, length, wide), bf),
+        vmem((chunks, length, wide), bf),
         vmem((length, 2 * state), bf),
         vmem((length, 2 * state), bf),
         vmem((length, heads), bf),
@@ -711,8 +753,9 @@
         vmem((m, length, 2 * heads), bf),
         vmem((n, heads, block), bf),
         vmem((n, heads, block), bf),
-        dma((n,)), dma((n,)), dma((m,)), dma((m,)), dma((m,)), dma((m,)),
-        dma((n,)), dma((n,)), dma((n,)), dma((n,)), dma((n,)), dma((n,)),
+        dma((n,)), dma((n,)), dma((m // 2, n)), dma((m // 2, n)), dma((m // 2, n)), dma((m // 2, n)),
+        dma((m,)), dma((m,)),
+        dma((chunks, n)), dma((chunks, n)), dma((n,)), dma((n,)), dma((n,)), dma((n,)),
         dma((chunks,)), dma((chunks,)), dma((chunks,)), dma((chunks,)),
         dma((n, m)), dma((n, m)), dma((n,)), dma((n,)), dma((9,)),
     ]
@@ -743,7 +786,11 @@
         out_grad[0],
     )
     head_grad, grad_b, grad_c, weight_grad = pl.pallas_call(
-        hand_over, out_shape=results, in_specs=[whole] * 4, out_specs=(whole,) * 4
+        hand_over,
+        out_shape=results,
+        in_specs=[whole] * 4,
+        out_specs=(pl.BlockSpec(memory_space=pltpu.HBM),) * 4,
+        scratch_shapes=[dma((4,))],
     )(*grads)
     return head_grad[None], grad_b.T[None], grad_c.T[None], weight_grad.T
 

time: 57.2 us -> 54.8 us (0.958)
  Pallas kernels: 56.4 us -> 54 us
    pallas_call x1, Pallas kernels: 54.5 us -> 52.1 us  [on_device_fused(): pl.pallas_call(functools.partial(layer_kernel, dims), out_shape=results,...]
where the time goes in v3:
time: 54.8 us; the launch traced here: 54.6 us
  Pallas kernels  54 us (99%)
  between operations  0.64 us (1%)
    pallas_call x1, Pallas kernels, on_device_fused(): pl.pallas_call(functools.partial(layer_kernel, dims), out_shape=results,...  52.1 us
    pallas_call x1, Pallas kernels, on_device_fused(): pl.pallas_call(hand_over, out_shape=results, in_specs=[whole] * 4, out_sp...  1.92 us

profile of v3, /device:TPU:0, one launch (start us, length us, event | category | flops | bytes accessed | tf_op | source)
XLA Modules:
  0.0 54.6 jit_solution(1111265834788159000)
XLA Ops:
  0.6 52.1 %shard_map.120 = (bf16[128,2048]{1,0:T(8,128)(2,1)}, f32[64,128]{1,0:T(8,128)}, f32[64,128]{1,0:T(8,128)}, f32[64,256]{1,0:T(8,128)}) custom-call(bf16[128,4096]{1,0:T(8,128)(2,1)} %bitcast.19, bf16[128,2048]{1,0:T(8,128)(2,1)} %bitcast.20, bf16[64,128]{1,0:T(8,128)(2,1)} %bitcast.23, bf16[64,128]{1,0:T(8,128)(2,1)} %bitcast.24, bf16[64,256]{1,0:T(8,128)(2,1)} %bitcast.22, ...), custom_call_target="tpu_custom_call" | custom-call | tf_op jit(solution)/shard_map/pallas_call | solution.py:768
  52.7 1.9 %shard_map.121 = (bf16[128,2048]{1,0:T(8,128)(2,1)}, f32[64,128]{1,0:T(8,128)}, f32[64,128]{1,0:T(8,128)}, f32[64,256]{1,0:T(8,128)}) custom-call(bf16[128,2048]{1,0:T(8,128)(2,1)} %get-tuple-element.12.refs_0_, f32[64,128]{1,0:T(8,128)} %get-tuple-element.13.refs_1_, f32[64,128]{1,0:T(8,128)} %get-tuple-element.14.refs_2_, f32[64,256]{1,0:T(8,128)} %get-tuple-element.15.refs_3_), custom_call_target="tpu_custom_call" | custom-call | tf_op jit(solution)/shard_map/pallas_call | solution.py:788

commit v4 on v3

--- a/solution.py
+++ b/solution.py
@@ -456,7 +456,6 @@
     step_wide[...] = expand(step)
     enter_wide[...] = expand(jnp.exp(cumul) * alive)
     leave_wide[...] = expand(jnp.exp(total - cumul) * tail)
-    eg[...] = (enter_wide[...] * g_ref[...].astype(f32)).astype(bf)
 
     f_copies = [
         remote(f_out.at[c], f_in.at[c], f_s.at[c], f_r.at[c], ctx=lax.rem(me + 1, n), dp=mine)
@@ -467,7 +466,10 @@
         for c in range(chunks)
     ]
     for c in range(chunks):
-        back_own[c] = mm(c_turn, eg[:, lanes(c)])
+        eg[:, lanes(c)], low = two_parts(
+            enter_wide[:, lanes(c)] * g_ref[:, lanes(c)].astype(f32)
+        )
+        back_own[c] = mm(c_turn, eg[:, lanes(c)]) + mm(c_turn, low)
 
         @pl.when(me == n - 1)
         def _():
@@ -546,10 +548,10 @@
         for copy in x_copies[c]:
             copy.wait_recv()
         xp[:, lanes(c)] = mm(p_recv, xr[c]).astype(bf)
-        lx[:, lanes(c)] = (
+        lx[:, lanes(c)], low = two_parts(
             leave_wide[:, lanes(c)] * step_wide[:, lanes(c)] * xp[:, lanes(c)].astype(f32)
-        ).astype(bf)
-        end_own[c] = mm(b_turn, lx[:, lanes(c)])
+        )
+        end_own[c] = mm(b_turn, lx[:, lanes(c)]) + mm(b_turn, low)
 
         @pl.when(me == 0)
         def _():
@@ -631,14 +633,17 @@
     for copy in g_copies:
         copy.wait_recv()
     eye_b = eye(2 * heads)
-    turned_grads = [nt(eye_b, gall[d]).astype(bf) for d in range(m)]
+    turned_grads = [
+        jnp.concatenate([nt(eye_b, gall[d + e]).astype(bf) for e in range(2)], axis=1)
+        for d in range(0, m, 2)
+    ]
 
     def weight_part(z):
         part = jnp.zeros((2 * heads, block), f32)
-        for d in range(m):
+        here = pl.ds(pl.multiple_of(z * block, block), block)
+        for d in range(0, m, 2):
             part = part + mm(
-                turned_grads[d],
-                uall[d, :, pl.ds(pl.multiple_of(z * block, block), block)],
+                turned_grads[d // 2], jnp.concatenate([uall[d, :, here], uall[d + 1, :, here]], axis=0)
             )
         return part[:heads] + part[heads:]
 

time: 54.8 us -> 55.1 us (level)
  no operation moved by 1% of the time
where the time goes in v4:
time: 55.1 us; the launch traced here: 55 us
  Pallas kernels  54.3 us (99%)
  between operations  0.64 us (1%)
    pallas_call x1, Pallas kernels, on_device_fused(): pl.pallas_call(functools.partial(layer_kernel, dims), out_shape=results,...  52.4 us
    pallas_call x1, Pallas kernels, on_device_fused(): pl.pallas_call(hand_over, out_shape=results, in_specs=[whole] * 4, out_sp...  1.92 us

profile of v4, /device:TPU:0, one launch (start us, length us, event | category | flops | bytes accessed | tf_op | source)
XLA Modules:
  0.0 55.0 jit_solution(8368834394737696418)
XLA Ops:
  0.6 52.4 %shard_map.120 = (bf16[128,2048]{1,0:T(8,128)(2,1)}, f32[64,128]{1,0:T(8,128)}, f32[64,128]{1,0:T(8,128)}, f32[64,256]{1,0:T(8,128)}) custom-call(bf16[128,4096]{1,0:T(8,128)(2,1)} %bitcast.19, bf16[128,2048]{1,0:T(8,128)(2,1)} %bitcast.20, bf16[64,128]{1,0:T(8,128)(2,1)} %bitcast.23, bf16[64,128]{1,0:T(8,128)(2,1)} %bitcast.24, bf16[64,256]{1,0:T(8,128)(2,1)} %bitcast.22, ...), custom_call_target="tpu_custom_call" | custom-call | tf_op jit(solution)/shard_map/pallas_call | solution.py:773
  53.0 1.9 %shard_map.121 = (bf16[128,2048]{1,0:T(8,128)(2,1)}, f32[64,128]{1,0:T(8,128)}, f32[64,128]{1,0:T(8,128)}, f32[64,256]{1,0:T(8,128)}) custom-call(bf16[128,2048]{1,0:T(8,128)(2,1)} %get-tuple-element.12.refs_0_, f32[64,128]{1,0:T(8,128)} %get-tuple-element.13.refs_1_, f32[64,128]{1,0:T(8,128)} %get-tuple-element.14.refs_2_, f32[64,256]{1,0:T(8,128)} %get-tuple-element.15.refs_3_), custom_call_target="tpu_custom_call" | custom-call | tf_op jit(solution)/shard_map/pallas_call | solution.py:793
